TPU v7x, 32 devices: a whole 2x2x4 slice. The times are simulated.
32 devices in a mesh: groups: 2 (over x), dp: 8 (over z, y), mat: 2 (over core).
Axes of the slice: x: 2, y: 2, z: 4, core: 2. Of those that a mesh axis runs over, the one named last changes fastest.
Arguments:
- in_factor: bfloat16 [256, 8, 64, 128], P(('groups', 'dp'), None, 'mat'), parts along dimension 0, may hold values from -6 to 6
- out_factor: bfloat16 [256, 8, 64, 128], P(('groups', 'dp')), parts along dimension 0, may hold values from -6 to 6
- seq_lengths: int32 [256], P(('groups', 'dp')), parts along dimension 0, may hold values from 1 to 128, 10240 in all
- sequence_ids: int32 [256], P('groups'), parts along dimension 0, may hold values from 0 to 127, each once
- matrix_owner: int32 [8], replicated, may hold values from 0 to 7, each once
- queries: bfloat16 [8, 512, 4096], P('dp', None, 'mat'), may hold values from -0.03125 to 0.03125
Outputs:
- fisher: bfloat16 [16, 4096, 4096], P(('groups', 'dp'), 'mat'), parts along dimension 0
- scores: float32 [256, 512], P(('groups', 'dp', 'mat')), parts along dimension 0
There are 2 independent parts, one for each index of `groups`. A program takes and returns all parts, laid end to end along the dimension named above; an argument that names none is the same for every part. Nothing has to cross between parts.
Inputs may be any that keep to these rules, and one draw needn't show every extreme that they name: `sequence_ids`: each value once. `matrix_owner`: each value once.
All inputs are finite; a program needn't handle non-finite values. No bound on the sum of `seq_lengths` on one device may be relied on, other than what follows from the above.
Results may differ from a plain program's by a relative error of at most 0.0057.
Values may be sent and summed in bfloat16 or wider, within the bound.
No kernel may reach another device: no remote copies, remote signals or barrier semaphores. Data moves between devices by JAX's collectives and lax.ppermute only.
A program may use at most 128 MiB of HBM per device.

v0:
```python
import jax
import jax.numpy as jnp
from jax import lax
from jax.sharding import PartitionSpec as P


def local(in_factor, out_factor, seq_lengths, sequence_ids, matrix_owner, queries):
    local_seqs, matrices, half_proj, length = in_factor.shape
    proj_width = out_factor.shape[2]
    half_width = half_proj * proj_width
    positions = jnp.arange(length, dtype=jnp.int32)
    token_mask = (positions[None, :] < seq_lengths[:, None]).astype(jnp.bfloat16)
    weighted = out_factor * token_mask[:, None, None, :]
    grad_tiles = jnp.einsum(
        "smit,smot->smio", in_factor, weighted, preferred_element_type=jnp.float32
    ) * length ** (-0.5)
    local_grads = grad_tiles.reshape(local_seqs, matrices, half_width).astype(jnp.bfloat16)
    slot_matrix = (
        jnp.zeros((matrices,), jnp.int32)
        .at[matrix_owner]
        .set(jnp.arange(matrices, dtype=jnp.int32))
    )
    whole_rows = lax.all_gather(local_grads, "mat", axis=2, tiled=True)
    ordered = jnp.take(whole_rows, slot_matrix, axis=1)
    full_rows = lax.all_to_all(ordered, "dp", split_axis=1, concat_axis=0, tiled=True)
    first_col = lax.axis_index("mat") * half_width
    own_half = lax.dynamic_slice_in_dim(full_rows, first_col, half_width, 2)
    total_seqs = full_rows.shape[0]
    products = jnp.einsum("rkj,rkl->kjl", own_half, full_rows, preferred_element_type=jnp.float32)
    fisher = (products / total_seqs).astype(jnp.bfloat16)
    inverse = (
        jnp.zeros((total_seqs,), jnp.int32)
        .at[sequence_ids]
        .set(jnp.arange(total_seqs, dtype=jnp.int32))
    )
    picked = jnp.take(own_half, inverse, axis=0)
    scores = lax.psum_scatter(
        jnp.einsum("rkj,kqj->rq", picked, queries, preferred_element_type=jnp.float32),
        ("dp", "mat"),
        scatter_dimension=0,
        tiled=True,
    )
    return (fisher, scores)


def solution(mesh):
    in_specs = (
        P(("groups", "dp"), None, "mat", None),
        P(("groups", "dp"), None, None, None),
        P(("groups", "dp")),
        P("groups"),
        P(),
        P("dp", None, "mat"),
    )
    out_specs = (P(("groups", "dp"), "mat", None), P(("groups", "dp", "mat"), None))
    return jax.shard_map(local, mesh=mesh, in_specs=in_specs, out_specs=out_specs, check_vma=False)
```

profile of v0, /device:TPU:0, one launch (start us, length us, event | category | flops | bytes accessed | tf_op | source)
XLA Modules:
  0.0 128.1 jit_solution(1983858971100439209)
XLA Ops:
  7.2 0.0 copy-start
  7.2 0.0 all-gather.2.cloned.1.call-start
  7.2 0.9 fusion.14
  8.1 4.0 %fusion.7 = bf16[16,8,32,64]{3,2,1,0:T(8,128)(2,1)} fusion(bf16[16,8,32,128]{3,2,1,0:T(8,128)(2,1)} %param.6, bf16[16,8,64,128]{3,2,1,0:T(8,128)(2,1)} %param.7, bf16[16,128]{1,0:T(8,128)(2,1)S(1)} %fusion.14), kind=kOutput, calls=%fused_computation.11 | convolution fusion | flops 68681728 | bytes 3674112 | tf_op jit(solution)/shard_map/smit,smot->smio/dot_general | solution.py:14
  12.1 0.0 copy-start.2
  12.1 2.1 %convert_element_type.25 = bf16[16,8,2048]{2,1,0:T(8,128)(2,1)S(1)} reshape(bf16[16,8,32,64]{3,2,1,0:T(8,128)(2,1)} %fusion.7) | data formatting | bytes 1048576 | tf_op jit(solution)/shard_map/convert_element_type | solution.py:17
  14.2 1.1 copy.8
  15.3 0.0 all-gather.2.cloned.1.call-update
  15.3 0.0 copy-done.2
  15.3 0.6 scatter_custom_fusion
  16.0 11.2 %all-gather.2.cloned.1.call-done = bf16[16,8,4096]{2,0,1:T(8,128)(2,1)} async-done(((bf16[16,8,2048]{2,0,1:T(8,128)(2,1)}), bf16[16,8,4096]{2,0,1:T(8,128)(2,1)}) %all-gather.2.cloned.1.call-update) | async-done | bytes 1048592 | tf_op jit(solution)/shard_map/all_gather | solution.py:23
  27.2 1.8 %gather_fusion = bf16[8,16,4096]{2,1,0:T(8,128)(2,1)S(1)} fusion(bf16[16,8,4096]{2,0,1:T(8,128)(2,1)} %all-gather.2.cloned.1.call-done, s32[1024]{0:T(1024)S(1)} %pad_clamp_fusion.1), kind=kCustom, calls=%fused_computation | custom fusion | bytes 2097184 | tf_op jit(solution)/shard_map/jit(_take)/gather | solution.py:24
  29.1 0.0 copy-start.3
  29.1 1.1 select_bitcast_fusion
  30.2 5.8 %all-to-all-start = ((bf16[16,8,4096]{2,0,1:T(8,128)(2,1)}), bf16[16,8,4096]{2,0,1:T(8,128)(2,1)S(1)}, u32[]{:S(2)}, u32[]{:S(2)}) async-start(bf16[16,8,4096]{2,0,1:T(8,128)(2,1)} %select_bitcast_fusion), calls=%async_computation | async-start | bytes 2097152 | tf_op jit(solution)/shard_map/all_to_all | solution.py:25
  36.0 0.0 reduce-scatter.2.cloned.1.call-start
  36.0 0.0 copy-done.3
  36.0 1.0 scatter_custom_fusion.1
  37.1 25.1 %all-to-all-done = bf16[16,8,4096]{2,0,1:T(8,128)(2,1)S(1)} async-done(((bf16[16,8,4096]{2,0,1:T(8,128)(2,1)}), bf16[16,8,4096]{2,0,1:T(8,128)(2,1)S(1)}, u32[]{:S(2)}, u32[]{:S(2)}) %all-to-all-start) | async-done | bytes 1048608 | tf_op jit(solution)/shard_map/all_to_all | solution.py:25
  62.2 0.0 copy-start.1
  62.2 1.0 copy-done.1
  63.2 1.1 dynamic-slice_bitcast_fusion
  64.3 0.9 gather_fusion.1
  65.2 0.0 copy-done
  65.2 1.5 %fusion.1 = f32[128,512]{1,0:T(8,128)} fusion(bf16[1,512,2048]{2,1,0:T(8,128)(2,1)S(1)} %copy-done, bf16[128,2048]{1,0:T(8,128)(2,1)S(1)} %gather_fusion.1, pred[128]{0:T(512)(128)(4,1)S(1)} %compare_and_fusion), kind=kOutput, calls=%fused_computation.6 | convolution fusion | flops 268697600 | bytes 2883712 | tf_op jit(solution)/shard_map/rkj,kqj->rq/dot_general | solution.py:38
  66.7 0.0 reduce-scatter.2.cloned.1.call-update
  66.8 9.8 %fusion = bf16[1,2048,4096]{2,1,0:T(8,128)(2,1)} fusion(bf16[128,2048]{1,0:T(8,128)(2,1)S(1)} %dynamic-slice_bitcast_fusion, bf16[128,4096]{1,0:T(8,128)(2,1)} %bitcast.32), kind=kOutput, calls=%fused_computation.5 | convolution fusion | flops 2164260864 | bytes 18350080 | tf_op jit(solution)/shard_map/rkj,rkl->kjl/dot_general | solution.py:29
  76.5 44.7 %reduce-scatter.2.cloned.1.call-done = f32[8,512]{1,0:T(8,128)} async-done(((f32[128,512]{1,0:T(8,128)}), f32[8,512]{1,0:T(8,128)}) %reduce-scatter.2.cloned.1.call-update) | async-done | bytes 16400 | tf_op jit(solution)/shard_map/reduce_scatter | solution.py:37
  (10 shorter events, 0.0 us)
Async XLA Ops:
  7.2 58.0 %copy-start = (bf16[1,512,2048]{2,1,0:T(8,128)(2,1)S(1)}, bf16[1,512,2048]{2,1,0:T(8,128)(2,1)}, u32[]{:S(2)}) copy-start(bf16[1,512,2048]{2,1,0:T(8,128)(2,1)} %param.11) | copy-start | bytes 6291460
  7.2 20.0 %all-gather.2.cloned.1.call-start = ((), (), s32[]{:S(2)}) async-start(), calls=%async_computation.2 | async-start | bytes 1572864 | tf_op jit(solution)/shard_map/all_gather | solution.py:23
  12.1 3.2 %copy-start.2 = (s32[8]{0:T(128)S(1)}, s32[8]{0:T(128)}, u32[]{:S(2)}) copy-start(s32[8]{0:T(128)} %param.10) | copy-start | bytes 100
  29.1 7.0 %copy-start.3 = (s32[128]{0:T(128)S(1)}, s32[128]{0:T(128)}, u32[]{:S(2)}) copy-start(s32[128]{0:T(128)} %param.9) | copy-start | bytes 1540
  30.2 32.0 %all-to-all-start = ((bf16[16,8,4096]{2,0,1:T(8,128)(2,1)}), bf16[16,8,4096]{2,0,1:T(8,128)(2,1)S(1)}, u32[]{:S(2)}, u32[]{:S(2)}) async-start(bf16[16,8,4096]{2,0,1:T(8,128)(2,1)} %select_bitcast_fusion), calls=%async_computation | async-start | bytes 2097152 | tf_op jit(solution)/shard_map/all_to_all | solution.py:25
  36.0 85.3 %reduce-scatter.2.cloned.1.call-start = ((), (), s32[]{:S(2)}) async-start(), calls=%async_computation.3 | async-start | bytes 278528 | tf_op jit(solution)/shard_map/reduce_scatter | solution.py:37
  62.2 1.0 copy-start.1
Sparse Core Ops, SparseCore 0:
  15.4 11.7 all-gather.1
  66.9 54.3 reduce-scatter.1
where the time goes:
time: 128 us
  waiting for transfers between devices  81.1 us (63%)
  matrix products  15.3 us (12%)
  between operations  14.2 us (11%)
  local copies, waits for them, and re-layouts  9.57 us (7%)
  starting transfers between devices  5.84 us (5%)
  other arithmetic  2.04 us (2%)
    reduce_scatter x1, waiting for transfers between devices, local(): lax.psum_scatter(jnp.einsum('rkj,kqj->rq', picked, queries, preferred_ele...  44.7 us
    all_to_all x1, waiting for transfers between devices, local(): lax.all_to_all(ordered, 'dp', split_axis=1, concat_axis=0, tiled=True)  25.1 us
    all_gather x1, waiting for transfers between devices, local(): whole_rows = lax.all_gather(local_grads, 'mat', axis=2, tiled=True)  11.2 us
    dot_general x1, matrix products, local(): jnp.einsum('rkj,rkl->kjl', own_half, full_rows, preferred_element_type=jn...  9.77 us
    all_to_all x1, starting transfers between devices, local(): lax.all_to_all(ordered, 'dp', split_axis=1, concat_axis=0, tiled=True)  5.77 us
    dot_general x1, matrix products, local(): jnp.einsum('smit,smot->smio', in_factor, weighted, preferred_element_type...  4.04 us
    convert_element_type x2, local copies, waits for them, and re-layouts, local(): grad_tiles.reshape(local_seqs, matrices, half_width).astype(jnp.bfloat16)  3.15 us
  transfers between devices with their start and end apart: 3, of which 3 were waited for; matrix products, arithmetic and copies ran while one was open for 9% of the time, Pallas kernels for 0%

commit v1 on v0

v1 whole, which is shorter than its diff:
```python
import functools

import jax
import jax.numpy as jnp
from jax import lax
from jax.experimental import pallas as pl
from jax.experimental.pallas import tpu as pltpu
from jax.sharding import PartitionSpec as P

NT = (((1,), (1,)), ((), ()))
TN = (((0,), (0,)), ((), ()))


def grad_body(owner, lengths, in_ref, out_ref, grad_ref, tiles):
    seqs, _, rows, length = in_ref.shape
    width = out_ref.shape[2]
    per = length // width
    scale = length ** (-0.5)
    lane = lax.broadcasted_iota(jnp.int32, (1, length), 1)
    for s in range(seqs):
        left = jnp.where(lane < lengths[s], in_ref[s, 0], 0)
        right = out_ref[s, 0]
        right = jnp.concatenate([right] * per, axis=0)
        tiles[s * rows:(s + 1) * rows, :] = lax.dot_general(
            left, right, NT, preferred_element_type=jnp.float32
        )
    for t in range(rows // per):
        tile = tiles[pl.ds(per * t, seqs, stride=rows), :]
        for p in range(1, per):
            other = tiles[pl.ds(per * t + p, seqs, stride=rows), :]
            tile = jnp.where(lane < p * width, tile, other)
        grad_ref[0, :, t * length:(t + 1) * length] = (tile * scale).astype(grad_ref.dtype)


def gradients(in_factor, out_factor, seq_lengths, matrix_owner):
    seqs, matrices, rows, length = in_factor.shape
    width = out_factor.shape[2]
    return pl.pallas_call(
        grad_body,
        out_shape=jax.ShapeDtypeStruct((matrices, seqs, rows * width), jnp.bfloat16),
        grid_spec=pltpu.PrefetchScalarGridSpec(
            num_scalar_prefetch=2,
            grid=(matrices,),
            in_specs=[
                pl.BlockSpec((seqs, 1, rows, length), lambda m, owner, lens: (0, m, 0, 0)),
                pl.BlockSpec((seqs, 1, width, length), lambda m, owner, lens: (0, m, 0, 0)),
            ],
            out_specs=pl.BlockSpec((1, seqs, rows * width), lambda m, owner, lens: (owner[m], 0, 0)),
            scratch_shapes=[pltpu.VMEM((seqs * rows, length), jnp.float32)],
        ),
        compiler_params=pltpu.CompilerParams(vmem_limit_bytes=32 << 20),
        name="gradients",
    )(matrix_owner, seq_lengths, in_factor, out_factor)


def score_body(rows_each, first, cores, core, ids, x_ref, q_ref, *refs):
    s_ref = refs[-1]
    rows = s_ref.shape[0]
    total = ids.shape[1]

    @pl.when(pl.program_id(0) == 0)
    def _():
        s_ref[...] = jnp.zeros_like(s_ref) if first else refs[0][...]

    at = lax.broadcasted_iota(jnp.int32, (rows, total), 0)
    wanted = (at // rows_each * cores + core[0]) * rows_each + at % rows_each
    pick = jnp.where(wanted == ids[...], 1.0, 0.0).astype(jnp.bfloat16)
    picked = jnp.dot(pick, x_ref[...], preferred_element_type=jnp.float32).astype(jnp.bfloat16)
    s_ref[...] += lax.dot_general(picked, q_ref[...], NT, preferred_element_type=jnp.float32)


def partial_scores(core, ids, x, q, before, rows, rows_each, cores):
    total, half = x.shape
    queries = q.shape[0]
    step = 512 if half % 512 == 0 else half
    whole = pl.BlockSpec((rows, queries), lambda k, core: (0, 0))
    extra = () if before is None else (before,)
    return pl.pallas_call(
        functools.partial(score_body, rows_each, before is None, cores),
        out_shape=jax.ShapeDtypeStruct((rows, queries), jnp.float32),
        grid_spec=pltpu.PrefetchScalarGridSpec(
            num_scalar_prefetch=1,
            grid=(half // step,),
            in_specs=[
                pl.BlockSpec((1, total), lambda k, core: (0, 0)),
                pl.BlockSpec((total, step), lambda k, core: (0, k)),
                pl.BlockSpec((queries, step), lambda k, core: (0, k)),
            ]
            + [whole] * len(extra),
            out_specs=whole,
        ),
        compiler_params=pltpu.CompilerParams(vmem_limit_bytes=32 << 20),
        cost_estimate=pl.CostEstimate(
            flops=2 * rows * queries * half, bytes_accessed=2 * half * (queries + total), transcendentals=0
        ),
        name="scores",
    )(core, ids, x, q, *extra)


def fisher_body(total, core, left_ref, own_ref, other_ref, f_ref):
    half = own_ref.shape[1]
    step = 1024 if half % 1024 == 0 else half
    for place, ref in ((core[0], own_ref), (1 - core[0], other_ref)):
        for at in range(0, half, step):
            block = lax.dot_general(
                left_ref[...], ref[:, at:at + step], TN, preferred_element_type=jnp.float32
            )
            where = pl.ds(pl.multiple_of(place * half + at, 128), step)
            f_ref[0, :, where] = (block * (1.0 / total)).astype(f_ref.dtype)


def fisher_block(core, own, other):
    total, half = own.shape
    step = 256 if half % 256 == 0 else half
    return pl.pallas_call(
        functools.partial(fisher_body, total),
        out_shape=jax.ShapeDtypeStruct((1, half, 2 * half), jnp.bfloat16),
        grid_spec=pltpu.PrefetchScalarGridSpec(
            num_scalar_prefetch=1,
            grid=(half // step,),
            in_specs=[
                pl.BlockSpec((total, step), lambda r, core: (0, r)),
                pl.BlockSpec((total, half), lambda r, core: (0, 0)),
                pl.BlockSpec((total, half), lambda r, core: (0, 0)),
            ],
            out_specs=pl.BlockSpec((1, step, 2 * half), lambda r, core: (0, r, 0)),
        ),
        compiler_params=pltpu.CompilerParams(vmem_limit_bytes=48 << 20),
        cost_estimate=pl.CostEstimate(
            flops=4 * total * half * half, bytes_accessed=4 * half * (half + total), transcendentals=0
        ),
        name="fisher",
    )(core, own, own, other)


def local(dp, cores, in_factor, out_factor, seq_lengths, sequence_ids, matrix_owner, queries):
    swap = [(c, (c + 1) % cores) for c in range(cores)]
    core = lax.axis_index("mat").astype(jnp.int32)[None]
    own_q = queries[0]
    other_q = lax.ppermute(own_q, "mat", swap)
    grads = gradients(in_factor, out_factor, seq_lengths, matrix_owner)
    seqs, half = grads.shape[1:]
    own = lax.all_to_all(grads, "dp", split_axis=0, concat_axis=0, tiled=True)
    total = dp * seqs
    own = own.reshape(total, half)
    other = lax.ppermute(own, "mat", swap)
    rows = total // cores
    rows_each = rows // dp
    ids = sequence_ids[None, :]
    part = partial_scores(core, ids, own, own_q, None, rows, rows_each, cores)
    part = partial_scores(core, ids, other, other_q, part, rows, rows_each, cores)
    parts = lax.all_to_all(part.reshape(dp, rows_each, -1), "dp", split_axis=0, concat_axis=0, tiled=True)
    fisher = fisher_block(core, own, other)
    return (fisher, jnp.sum(parts, axis=0))


def solution(mesh):
    in_specs = (
        P(("groups", "dp"), None, "mat", None),
        P(("groups", "dp"), None, None, None),
        P(("groups", "dp")),
        P("groups"),
        P(),
        P("dp", None, "mat"),
    )
    out_specs = (P(("groups", "dp"), "mat", None), P(("groups", "dp", "mat"), None))
    body = functools.partial(local, mesh.shape["dp"], mesh.shape["mat"])
    return jax.shard_map(body, mesh=mesh, in_specs=in_specs, out_specs=out_specs, check_vma=False)
```

time: 128 us -> 50.9 us (0.40)
  waiting for transfers between devices: 81.1 us -> 0.23 us
  blocking collectives: 0 us -> 21.7 us
  Pallas kernels: 0 us -> 18.9 us
  matrix products: 15.3 us -> 0 us
  between operations: 14.2 us -> 0.67 us
  local copies, waits for them, and re-layouts: 9.57 us -> 4.24 us
  starting transfers between devices: 5.84 us -> 4.16 us
  other arithmetic: 2.04 us -> 0.62 us
    reduce_scatter x1 -> x0, waiting for transfers between devices: 44.7 us -> none  [local(): lax.psum_scatter(jnp.einsum('rkj,kqj->rq', picked, queries, preferred_ele...]
    all_to_all x1, waiting for transfers between devices: 25.1 us -> 0.01 us  [local(): lax.all_to_all(part.reshape(dp, rows_each, -1), 'dp', split_axis=0, conca...]
    all_to_all x0 -> x1, blocking collectives: none -> 21.7 us  [local(): own = lax.all_to_all(grads, 'dp', split_axis=0, concat_axis=0, tiled=True)]
    pallas_call x0 -> x4, Pallas kernels: none -> 18.9 us  [the longest x1 9 us: fisher_block(): pl.pallas_call(functools.partial(fisher_body, total), out_shape=jax.Shape...]
    dot_general x3 -> x0, matrix products: 15.3 us -> none  [the longest x1 9.77 us: local(): jnp.einsum('rkj,rkl->kjl', own_half, full_rows, preferred_element_type=jn...]
    all_gather x1 -> x0, waiting for transfers between devices: 11.2 us -> none  [local(): whole_rows = lax.all_gather(local_grads, 'mat', axis=2, tiled=True)]
    unnamed x8 -> x12, local copies, waits for them, and re-layouts: 0.99 us -> 4.24 us
    convert_element_type x2 -> x0, local copies, waits for them, and re-layouts: 3.15 us -> none  [local(): grad_tiles.reshape(local_seqs, matrices, half_width).astype(jnp.bfloat16)]
  transfers between devices with their start and end apart: 3 -> 3, of which waited for: 3 -> 1; matrix products, arithmetic and copies ran while one was open for 9% -> 0% of each run, Pallas kernels for 0% -> 30%
where the time goes in v1:
time: 50.9 us; the launch traced here: 50.5 us
  blocking collectives  21.7 us (43%)
  Pallas kernels  18.9 us (37%)
  local copies, waits for them, and re-layouts  4.24 us (8%)
  starting transfers between devices  4.16 us (8%)
  between operations  0.67 us (1%)
  other arithmetic  0.62 us (1%)
    all_to_all x1, blocking collectives, local(): own = lax.all_to_all(grads, 'dp', split_axis=0, concat_axis=0, tiled=True)  21.7 us
    pallas_call x1, Pallas kernels, fisher_block(): pl.pallas_call(functools.partial(fisher_body, total), out_shape=jax.Shape...  9 us
    pallas_call x2, Pallas kernels, partial_scores(): pl.pallas_call(functools.partial(score_body, rows_each, before is None, c...  5.53 us
    pallas_call x1, Pallas kernels, gradients(): pl.pallas_call(grad_body, out_shape=jax.ShapeDtypeStruct((matrices, seqs,...  4.41 us
    unnamed x12, local copies, waits for them, and re-layouts  4.24 us
    all_to_all x1, starting transfers between devices, local(): lax.all_to_all(part.reshape(dp, rows_each, -1), 'dp', split_axis=0, conca...  3.64 us
  transfers between devices with their start and end apart: 3, of which 1 were waited for; matrix products, arithmetic and copies ran while one was open for 0% of the time, Pallas kernels for 30%

profile of v1, /device:TPU:0, one launch (start us, length us, event | category | flops | bytes accessed | tf_op | source)
XLA Modules:
  0.0 50.5 jit_solution(5938713803766298595)
XLA Ops:
  0.6 0.0 copy-start
  0.6 0.5 %collective-permute-start.1 = (bf16[512,2048]{1,0:T(8,128)(2,1)}, bf16[512,2048]{1,0:T(8,128)(2,1)}, u32[]{:S(2)}, u32[]{:S(2)}) collective-permute-start(bf16[512,2048]{1,0:T(8,128)(2,1)} %bitcast.9), channel_id=1, source_target_pairs={{0,1},{1,0},{2,3},{3,2},{4,5},{5,4},{6,7},{7,6},{8,9},{9,8},{10,11... | collective-permute-start | bytes 6291464 | tf_op jit(solution)/shard_map/ppermute | solution.py:140
  1.2 0.0 copy-start.1
  1.2 1.7 %copy-done.1 = bf16[16,8,64,128]{3,2,1,0:T(8,128)(2,1)S(1)} copy-done((bf16[16,8,64,128]{3,2,1,0:T(8,128)(2,1)S(1)}, bf16[16,8,64,128]{3,2,1,0:T(8,128)(2,1)}, u32[]{:S(2)}) %copy-start.1) | copy-done | bytes 2097176
  2.9 0.0 copy-start.2
  2.9 1.2 %copy-done.2 = bf16[16,8,32,128]{3,2,1,0:T(8,128)(2,1)S(1)} copy-done((bf16[16,8,32,128]{3,2,1,0:T(8,128)(2,1)S(1)}, bf16[16,8,32,128]{3,2,1,0:T(8,128)(2,1)}, u32[]{:S(2)}) %copy-start.2) | copy-done | bytes 1048600
  4.1 0.0 copy-start.4
  4.1 0.7 %copy-done.4 = s32[8]{0:T(128)S(1)} copy-done((s32[8]{0:T(128)S(1)}, s32[8]{0:T(128)}, u32[]{:S(2)}) %copy-start.4) | copy-done | bytes 56
  4.7 0.0 copy-start.5
  4.7 0.7 %copy-done.5 = s32[16]{0:T(128)S(1)} copy-done((s32[16]{0:T(128)S(1)}, s32[16]{0:T(128)}, u32[]{:S(2)}) %copy-start.5) | copy-done | bytes 88
  5.4 0.0 copy-start.3
  5.4 4.4 %gradients.1 = bf16[8,16,2048]{2,1,0:T(8,128)(2,1)S(1)} custom-call(s32[8]{0:T(128)S(1)} %copy-done.4, s32[16]{0:T(128)S(1)} %copy-done.5, bf16[16,8,32,128]{3,2,1,0:T(8,128)(2,1)S(1)} %copy-done.2, bf16[16,8,64,128]{3,2,1,0:T(8,128)(2,1)S(1)} %copy-done.1), custom_call_target="tpu_custom_call" | custom-call | tf_op jit(solution)/shard_map/gradients/pallas_call | solution.py:38
  9.8 21.7 %all_to_all.10 = bf16[8,16,2048]{2,1,0:T(8,128)(2,1)S(1)} all-to-all(bf16[8,16,2048]{2,1,0:T(8,128)(2,1)S(1)} %gradients.1), channel_id=1, replica_groups=mesh['groups'=2,'dp'=8,'mat'=2] {'dp'}, dimensions={0} | all-to-all | bytes 1048576 | tf_op jit(solution)/shard_map/all_to_all | solution.py:143
  31.5 0.0 collective-permute-start
  31.5 0.0 copy-done
  31.5 0.0 copy-done.3
  31.5 1.7 %scores.2.refs_0_ = f32[64,512]{1,0:T(8,128)S(1)} custom-call(s32[1]{0:T(128)} %bitcast.core, s32[1,128]{1,0:T(1,128)S(1)} %bitcast.11, bf16[128,2048]{1,0:T(8,128)(2,1)S(1)} %bitcast.6, bf16[512,2048]{1,0:T(8,128)(2,1)S(1)} %bitcast.10), custom_call_target="tpu_custom_call" | custom-call | flops 134217728 | bytes 2621440 | tf_op jit(solution)/shard_map/scores/pallas_call | solution.py:78
  33.2 0.2 collective-permute-done.other_ref.x_ref
  33.4 0.0 collective-permute-done.1.q_ref
  33.4 3.9 %scores.3 = f32[64,512]{1,0:T(8,128)} custom-call(s32[1]{0:T(128)} %bitcast.core, s32[1,128]{1,0:T(1,128)S(1)} %bitcast.12, bf16[128,2048]{1,0:T(8,128)(2,1)S(1)} %collective-permute-done.other_ref.x_ref, bf16[512,2048]{1,0:T(8,128)(2,1)} %collective-permute-done.1.q_ref, f32[64,512]{1,0:T(8,128)S(1)} %scores.2.refs_0_), custom_call_target="tpu_custom_call" | custom-call | flops 134217728 | bytes 2621440 | tf_op jit(solution)/shard_map/scores/pallas_call | solution.py:78
  37.3 3.6 %all-to-all-start.1 = ((f32[8,8,512]{2,1,0:T(8,128)}), f32[8,8,512]{2,1,0:T(8,128)S(1)}, u32[]{:S(2)}, u32[]{:S(2)}) async-start(f32[8,8,512]{2,1,0:T(8,128)} %bitcast.4), calls=%async_computation.1 | async-start | bytes 262144 | tf_op jit(solution)/shard_map/all_to_all | solution.py:152
  40.9 9.0 %fisher.1 = bf16[1,2048,4096]{2,1,0:T(8,128)(2,1)} custom-call(s32[1]{0:T(128)} %bitcast.core, bf16[128,2048]{1,0:T(8,128)(2,1)S(1)} %bitcast.7, bf16[128,2048]{1,0:T(8,128)(2,1)S(1)} %bitcast.8, bf16[128,2048]{1,0:T(8,128)(2,1)S(1)} %collective-permute-done.other_ref.x_ref), custom_call_target="tpu_custom_call" | custom-call | flops 2147483648 | bytes 17825792 | tf_op jit(solution)/shard_map/fisher/pallas_call | solution.py:115
  49.9 0.0 all-to-all-done.1
  49.9 0.6 %reduce_sum.9 = f32[8,512]{1,0:T(8,128)} reduce(f32[8,8,512]{2,1,0:T(8,128)S(1)} %all-to-all-done.1, f32[]{:T(128)} %constant.1.clone.1), dimensions={0}, to_apply=%region_0.0 | reduce | flops 28672 | bytes 147460 | tf_op jit(solution)/shard_map/reduce_sum | solution.py:154
Async XLA Ops:
  0.6 30.9 %copy-start = (bf16[1,512,2048]{2,1,0:T(8,128)(2,1)S(1)}, bf16[1,512,2048]{2,1,0:T(8,128)(2,1)}, u32[]{:S(2)}) copy-start(bf16[1,512,2048]{2,1,0:T(8,128)(2,1)} %param.11) | copy-start | bytes 6291460
  0.6 32.8 %collective-permute-start.1 = (bf16[512,2048]{1,0:T(8,128)(2,1)}, bf16[512,2048]{1,0:T(8,128)(2,1)}, u32[]{:S(2)}, u32[]{:S(2)}) collective-permute-start(bf16[512,2048]{1,0:T(8,128)(2,1)} %bitcast.9), channel_id=1, source_target_pairs={{0,1},{1,0},{2,3},{3,2},{4,5},{5,4},{6,7},{7,6},{8,9},{9,8},{10,11... | collective-permute-start | bytes 6291464 | tf_op jit(solution)/shard_map/ppermute | solution.py:140
  1.2 1.7 %copy-start.1 = (bf16[16,8,64,128]{3,2,1,0:T(8,128)(2,1)S(1)}, bf16[16,8,64,128]{3,2,1,0:T(8,128)(2,1)}, u32[]{:S(2)}) copy-start(bf16[16,8,64,128]{3,2,1,0:T(8,128)(2,1)} %out_ref.1) | copy-start | bytes 6291460
  2.9 1.2 %copy-start.2 = (bf16[16,8,32,128]{3,2,1,0:T(8,128)(2,1)S(1)}, bf16[16,8,32,128]{3,2,1,0:T(8,128)(2,1)}, u32[]{:S(2)}) copy-start(bf16[16,8,32,128]{3,2,1,0:T(8,128)(2,1)} %in_ref.1) | copy-start | bytes 3145732
  4.1 0.7 %copy-start.4 = (s32[8]{0:T(128)S(1)}, s32[8]{0:T(128)}, u32[]{:S(2)}) copy-start(s32[8]{0:T(128)} %owner.1) | copy-start | bytes 100
  4.7 0.7 %copy-start.5 = (s32[16]{0:T(128)S(1)}, s32[16]{0:T(128)}, u32[]{:S(2)}) copy-start(s32[16]{0:T(128)} %lengths.1) | copy-start | bytes 196
  5.4 26.1 %copy-start.3 = (s32[128]{0:T(128)S(1)}, s32[128]{0:T(128)}, u32[]{:S(2)}) copy-start(s32[128]{0:T(128)} %param.9) | copy-start | bytes 1540
  31.5 1.9 %collective-permute-start = (bf16[128,2048]{1,0:T(8,128)(2,1)S(1)}, bf16[128,2048]{1,0:T(8,128)(2,1)S(1)}, u32[]{:S(2)}, u32[]{:S(2)}) collective-permute-start(bf16[128,2048]{1,0:T(8,128)(2,1)S(1)} %bitcast.5), channel_id=1, source_target_pairs={{0,1},{1,0},{2,3},{3,2},{4,5},{5,4},{6,7},{7,6},{8,9},{9,8},{10,11... | collective-permute-start | bytes 1572872 | tf_op jit(solution)/shard_map/ppermute | solution.py:146
  37.3 12.6 %all-to-all-start.1 = ((f32[8,8,512]{2,1,0:T(8,128)}), f32[8,8,512]{2,1,0:T(8,128)S(1)}, u32[]{:S(2)}, u32[]{:S(2)}) async-start(f32[8,8,512]{2,1,0:T(8,128)} %bitcast.4), calls=%async_computation.1 | async-start | bytes 262144 | tf_op jit(solution)/shard_map/all_to_all | solution.py:152

commit v2 on v0

v2 whole, which is shorter than its diff:
```python
import functools

import jax
import jax.numpy as jnp
from jax import lax
from jax.experimental import pallas as pl
from jax.experimental.pallas import tpu as pltpu
from jax.sharding import PartitionSpec as P

NT = (((1,), (1,)), ((), ()))
TN = (((0,), (0,)), ((), ()))
VMEM = pl.BlockSpec(memory_space=pltpu.VMEM)
SMEM = pl.BlockSpec(memory_space=pltpu.SMEM)
HBM = pl.BlockSpec(memory_space=pl.ANY)


def here(x):
    return pltpu.with_memory_space_constraint(x, pltpu.VMEM)


def far(x):
    return pltpu.with_memory_space_constraint(x, pltpu.HBM)


def matrix_at(owner, slot):
    matrix = jnp.int32(0)
    for m in range(owner.shape[0]):
        matrix = jnp.where(owner[m] == slot, m, matrix)
    return matrix


def slot_rows(in_v, other_v, out_v, matrix, lengths, tiles, store):
    seqs, _, width, length = out_v.shape
    rows = 2 * in_v.shape[2]
    stride = tiles.shape[0] // seqs
    per = length // width
    scale = length ** (-0.5)
    lane = lax.broadcasted_iota(jnp.int32, (1, length), 1)
    for s in range(seqs):
        left = jnp.concatenate([in_v[s, matrix], other_v[s, matrix]], axis=0)
        left = jnp.where(lane < lengths[s], left, 0)
        tile = lax.dot_general(left, out_v[s, matrix], NT, preferred_element_type=jnp.float32)
        tiles[s * stride:s * stride + rows, :] = jnp.concatenate([tile] * per, axis=1)
    for t in range(rows // per):
        tile = tiles[pl.ds(per * t, seqs, stride=stride), :]
        for p in range(1, per):
            other = tiles[pl.ds(per * t + p, seqs, stride=stride), :]
            tile = jnp.where(lane < p * width, tile, other)
        store(t * length, (tile * scale).astype(jnp.bfloat16))


def load_body(*refs):
    *refs, through, sem, out_sem = refs
    n = len(refs) // 2
    parts = sem.shape[1]

    def copies(source, target, sems):
        each = source.shape[0] // parts
        return [
            pltpu.make_async_copy(source.at[pl.ds(j * each, each)], target.at[pl.ds(j * each, each)], sems.at[j])
            for j in range(parts)
        ]

    inward = copies(refs[n - 1], through, sem.at[n - 1])
    outward = copies(through, refs[2 * n - 1], out_sem)
    near = [copies(refs[i], refs[n + i], sem.at[i]) for i in range(n - 1)]
    for copy in inward + sum(near, []):
        copy.start()
    for one, two in zip(inward, outward):
        one.wait()
        two.start()
    for copy in sum(near, []) + outward:
        copy.wait()


def load(near, distant):
    arrays = (*near, distant)
    parts = 4 if distant.shape[0] % 64 == 0 and all(a.shape[0] % 4 == 0 for a in near) else 1
    return pl.pallas_call(
        load_body,
        out_shape=[pltpu.VMEM(a.shape, a.dtype) for a in near] + [pltpu.HBM(distant.shape, distant.dtype)],
        in_specs=[HBM] * len(arrays),
        out_specs=[VMEM] * len(near) + [HBM],
        scratch_shapes=[
            pltpu.VMEM(distant.shape, distant.dtype),
            pltpu.SemaphoreType.DMA((len(arrays), parts)),
            pltpu.SemaphoreType.DMA((parts,)),
        ],
        compiler_params=pltpu.CompilerParams(vmem_limit_bytes=4 << 20),
        name="load",
    )(*[far(a) for a in arrays])


def whole_body(pairs, owner, me, core, lengths, in_v, other_v, out_v, _, *refs):
    grads, tiles = refs[:len(pairs)], refs[-1]
    half = grads[0].shape[1] // 2
    for at, pair in enumerate(pairs):
        matrix = matrix_at(owner, me[0] ^ jnp.where(core[0] == 0, pair[0], pair[1]))

        def store(column, x):
            first = jnp.where(core[0] == 0, column, (column + half) % (2 * half))
            grads[at][:, pl.ds(pl.multiple_of(first, 128), x.shape[1])] = x

        slot_rows(in_v, other_v, out_v, matrix, lengths, tiles.at[at % 2], store)


def whole_slots(pairs, owner, me, core, lengths, in_v, other_in, out_v, passed):
    seqs, _, rows, length = in_v.shape
    width = out_v.shape[2]
    n = len(pairs)
    return pl.pallas_call(
        functools.partial(whole_body, pairs),
        out_shape=[pltpu.VMEM((seqs, 2 * rows * width), jnp.bfloat16)] * n
        + [pltpu.HBM(passed.shape, passed.dtype)],
        in_specs=[SMEM] * 4 + [VMEM] * 3 + [HBM],
        out_specs=[VMEM] * n + [HBM],
        input_output_aliases={7: n},
        scratch_shapes=[pltpu.VMEM((2, seqs * (2 * rows + 8), length), jnp.float32)],
        compiler_params=pltpu.CompilerParams(vmem_limit_bytes=12 << 20),
        cost_estimate=pl.CostEstimate(
            flops=4 * n * seqs * rows * width * length,
            bytes_accessed=2 * n * seqs * length * (2 * rows + width),
            transcendentals=0,
        ),
        name="whole_slots",
    )(far(owner), me, core, far(lengths), here(in_v), here(other_in), here(out_v), far(passed))


def score_body(pairs, rows_each, cores, core, me, ids, *refs):
    mine, theirs = refs[:len(pairs)], refs[len(pairs):2 * len(pairs)]
    own_q, other_q, s_ref, x_ref = refs[2 * len(pairs):]
    seqs, width = mine[0].shape
    half = width // 2
    rows = s_ref.shape[0]
    total = ids.shape[1]
    own_at = pl.ds(pl.multiple_of(core[0] * half, 128), half)
    other_at = pl.ds(pl.multiple_of((1 - core[0]) * half, 128), half)

    def place(k):
        return pl.ds(pl.multiple_of((me[0] ^ k) * seqs, 16), seqs)

    for pair, own, other in zip(pairs, mine, theirs):
        x_ref[place(jnp.where(core[0] == 0, pair[0], pair[1])), :] = own[...]
        x_ref[place(jnp.where(core[0] == 0, pair[1], pair[0])), :] = other[...]
    at = lax.broadcasted_iota(jnp.int32, (rows, total), 0)
    wanted = (at // rows_each * cores + core[0]) * rows_each + at % rows_each
    pick = jnp.where(wanted == ids[...], 1.0, 0.0).astype(jnp.bfloat16)
    for first, where, q_ref in ((True, own_at, own_q), (False, other_at, other_q)):
        picked = jnp.dot(pick, x_ref[:, where], preferred_element_type=jnp.float32).astype(jnp.bfloat16)
        part = lax.dot_general(picked, q_ref[...], NT, preferred_element_type=jnp.float32)
        s_ref[...] = part if first else s_ref[...] + part


def partial_scores(pairs, core, me, ids, mine, theirs, own_q, other_q):
    cores = 2
    seqs, width = mine[0].shape
    half = width // 2
    total = ids.shape[1]
    queries = own_q.shape[0]
    rows = total // cores
    rows_each = rows // (total // seqs)
    args = [*mine, *theirs, own_q, other_q]
    return pl.pallas_call(
        functools.partial(score_body, pairs, rows_each, cores),
        out_shape=[pltpu.VMEM((rows, queries), jnp.float32), pltpu.VMEM((total, 2 * half), jnp.bfloat16)],
        in_specs=[SMEM, SMEM] + [VMEM] * (1 + len(args)),
        out_specs=[VMEM] * 2,
        compiler_params=pltpu.CompilerParams(vmem_limit_bytes=16 << 20),
        cost_estimate=pl.CostEstimate(
            flops=4 * rows * queries * half, bytes_accessed=4 * half * (queries + total), transcendentals=0
        ),
        name="scores",
    )(core, me, ids, *[here(arg) for arg in args])


def fisher_body(total, core, x_ref, f_hbm, left, out, sem):
    half = x_ref.shape[1] // 2
    depth, block, _ = out.shape
    step = 512 if half % 512 == 0 else half
    for at in range(0, half, block):
        where = pl.ds(pl.multiple_of(core[0] * half + at, 128), block)
        left[at:at + block, :] = x_ref[:, where].T

    def copy(i):
        rows = pl.ds(pl.multiple_of(i * block, block), block)
        return pltpu.make_async_copy(out.at[i % depth], f_hbm.at[0, rows], sem.at[i % depth])

    @pl.loop(0, half // block)
    def _(i):
        @pl.when(i >= depth)
        def _():
            copy(i - depth).wait()

        rows = left[pl.ds(pl.multiple_of(i * block, block), block), :]
        for at in range(0, 2 * half, step):
            tile = jnp.dot(rows, x_ref[:, at:at + step], preferred_element_type=jnp.float32)
            out[i % depth, :, at:at + step] = (tile * (1.0 / total)).astype(out.dtype)
        copy(i).start()

    for i in range(half // block - depth, half // block):
        copy(i).wait()


def fisher_block(core, x):
    total, half = x.shape[0], x.shape[1] // 2
    block, depth = (256, 4) if half % 256 == 0 and half >= 1024 else (half, 1)
    return pl.pallas_call(
        functools.partial(fisher_body, total),
        out_shape=jax.ShapeDtypeStruct((1, half, 2 * half), jnp.bfloat16),
        in_specs=[SMEM, VMEM],
        out_specs=HBM,
        scratch_shapes=[
            pltpu.VMEM((half, total), jnp.bfloat16),
            pltpu.VMEM((depth, block, 2 * half), jnp.bfloat16),
            pltpu.SemaphoreType.DMA((depth,)),
        ],
        compiler_params=pltpu.CompilerParams(vmem_limit_bytes=24 << 20),
        cost_estimate=pl.CostEstimate(
            flops=4 * total * half * half, bytes_accessed=4 * half * (half + total), transcendentals=0
        ),
        name="fisher",
    )(core, here(x))


def local(dp, cores, in_factor, out_factor, seq_lengths, sequence_ids, matrix_owner, queries):
    assert cores == 2 and dp % 2 == 0 and dp & (dp - 1) == 0
    swap = [(0, 1), (1, 0)]
    core = lax.axis_index("mat").astype(jnp.int32)[None]
    me = lax.axis_index("dp").astype(jnp.int32)[None]
    other_in = lax.ppermute(in_factor, "mat", swap)
    own_q = queries[0]
    in_v, out_v, late_q = load((in_factor, out_factor), own_q)
    order = list(range(dp // 2, dp)) + list(range(1, dp // 2)) + [0]
    pairs = tuple(zip(order[::2], order[1::2]))
    *made, late_q = whole_slots(pairs, matrix_owner, me, core, seq_lengths, in_v, other_in, out_v, late_q)
    mine = [
        lax.ppermute(
            piece, ("dp", "mat"), [(d * 2 + c, (d ^ pair[c]) * 2 + c) for d in range(dp) for c in range(2)]
        )
        for pair, piece in zip(pairs, made)
    ]
    other_q = lax.ppermute(late_q, "mat", swap)
    theirs = [lax.ppermute(piece, "mat", swap) for piece in mine]
    part, x = partial_scores(pairs, core, me, sequence_ids[None, :], mine, theirs, own_q, other_q)
    parts = lax.all_to_all(
        part.reshape(dp, part.shape[0] // dp, -1), "dp", split_axis=0, concat_axis=0, tiled=True
    )
    fisher = fisher_block(core, x)
    return (fisher, jnp.sum(parts, axis=0))


def solution(mesh):
    in_specs = (
        P(("groups", "dp"), None, "mat", None),
        P(("groups", "dp"), None, None, None),
        P(("groups", "dp")),
        P("groups"),
        P(),
        P("dp", None, "mat"),
    )
    out_specs = (P(("groups", "dp"), "mat", None), P(("groups", "dp", "mat"), None))
    body = functools.partial(local, mesh.shape["dp"], mesh.shape["mat"])
    return jax.shard_map(body, mesh=mesh, in_specs=in_specs, out_specs=out_specs, check_vma=False)
```

time: 128 us -> 40.5 us (0.32)
  waiting for transfers between devices: 81.1 us -> 8.79 us
  matrix products: 15.3 us -> 0 us
  Pallas kernels: 0 us -> 14.6 us
  between operations: 14.2 us -> 0.71 us
  starting transfers between devices: 5.84 us -> 15.5 us
  local copies, waits for them, and re-layouts: 9.57 us -> 0.01 us
  other arithmetic: 2.04 us -> 0.62 us
    reduce_scatter x1 -> x0, waiting for transfers between devices: 44.7 us -> none  [local(): lax.psum_scatter(jnp.einsum('rkj,kqj->rq', picked, queries, preferred_ele...]
    all_to_all x1, waiting for transfers between devices: 25.1 us -> 0.35 us  [local(): lax.all_to_all(part.reshape(dp, part.shape[0] // dp, -1), 'dp', split_axi...]
    dot_general x3 -> x0, matrix products: 15.3 us -> none  [the longest x1 9.77 us: local(): jnp.einsum('rkj,rkl->kjl', own_half, full_rows, preferred_element_type=jn...]
    pallas_call x0 -> x4, Pallas kernels: none -> 14.6 us  [the longest x1 7.11 us: fisher_block(): pl.pallas_call(functools.partial(fisher_body, total), out_shape=jax.Shape...]
    all_gather x1 -> x0, waiting for transfers between devices: 11.2 us -> none  [local(): whole_rows = lax.all_gather(local_grads, 'mat', axis=2, tiled=True)]
    ppermute x0 -> x10, starting transfers between devices: none -> 10.2 us  [the longest x4 8.97 us: local(): lax.ppermute(piece, ('dp', 'mat'), [(d * 2 + c, (d ^ pair[c]) * 2 + c) fo...]
    ppermute x0 -> x10, waiting for transfers between devices: none -> 8.44 us  [the longest x4 7.1 us: local(): lax.ppermute(piece, ('dp', 'mat'), [(d * 2 + c, (d ^ pair[c]) * 2 + c) fo...]
    convert_element_type x2 -> x0, local copies, waits for them, and re-layouts: 3.15 us -> none  [local(): grad_tiles.reshape(local_seqs, matrices, half_width).astype(jnp.bfloat16)]
  transfers between devices with their start and end apart: 3 -> 11, of which waited for: 3 -> 4; matrix products, arithmetic and copies ran while one was open for 9% -> 0% of each run, Pallas kernels for 0% -> 26%
where the time goes in v2:
time: 40.5 us; the launch traced here: 40.3 us
  starting transfers between devices  15.5 us (38%)
  Pallas kernels  14.6 us (36%)
  waiting for transfers between devices  8.79 us (22%)
  between operations  0.71 us (2%)
  other arithmetic  0.62 us (2%)
    ppermute x4, starting transfers between devices, local(): lax.ppermute(piece, ('dp', 'mat'), [(d * 2 + c, (d ^ pair[c]) * 2 + c) fo...  8.97 us
    pallas_call x1, Pallas kernels, fisher_block(): pl.pallas_call(functools.partial(fisher_body, total), out_shape=jax.Shape...  7.11 us
    ppermute x4, waiting for transfers between devices, local(): lax.ppermute(piece, ('dp', 'mat'), [(d * 2 + c, (d ^ pair[c]) * 2 + c) fo...  7.1 us
    all_to_all x1, starting transfers between devices, local(): lax.all_to_all(part.reshape(dp, part.shape[0] // dp, -1), 'dp', split_axi...  5.3 us
    pallas_call x1, Pallas kernels, load(): pl.pallas_call(load_body, out_shape=[pltpu.VMEM(a.shape, a.dtype) for a i...  3.36 us
    pallas_call x1, Pallas kernels, partial_scores(): pl.pallas_call(functools.partial(score_body, pairs, rows_each, cores), ou...  2.31 us
    pallas_call x1, Pallas kernels, whole_slots(): pl.pallas_call(functools.partial(whole_body, pairs), out_shape=[pltpu.VME...  1.85 us
    ppermute x4, waiting for transfers between devices, local(): theirs = [lax.ppermute(piece, 'mat', swap) for piece in mine]  1.33 us
  transfers between devices with their start and end apart: 11, of which 4 were waited for; matrix products, arithmetic and copies ran while one was open for 0% of the time, Pallas kernels for 26%

profile of v2, /device:TPU:0, one launch (start us, length us, event | category | flops | bytes accessed | tf_op | source)
XLA Modules:
  0.0 40.3 jit_solution(4894360205739819330)
XLA Ops:
  0.6 0.5 %collective-permute-start = (bf16[16,8,32,128]{3,2,1,0:T(8,128)(2,1)}, bf16[16,8,32,128]{3,2,1,0:T(8,128)(2,1)S(1)}, u32[]{:S(2)}, u32[]{:S(2)}) collective-permute-start(bf16[16,8,32,128]{3,2,1,0:T(8,128)(2,1)} %refs_0_.1), channel_id=1, source_target_pairs={{0,1},{1,0},{2,3},{3,2},{4,5},{5,4},{6,7},{7,6},{8,9},{9,8},{10,11... | collective-permute-start | bytes 3145736 | tf_op jit(solution)/shard_map/ppermute | solution.py:230
  1.1 3.4 %load.1 = (bf16[16,8,32,128]{3,2,1,0:T(8,128)(2,1)S(1)}, bf16[16,8,64,128]{3,2,1,0:T(8,128)(2,1)S(1)}, bf16[512,2048]{1,0:T(8,128)(2,1)}) custom-call(bf16[16,8,32,128]{3,2,1,0:T(8,128)(2,1)} %refs_0_.1, bf16[16,8,64,128]{3,2,1,0:T(8,128)(2,1)} %refs_1_.1, bf16[512,2048]{1,0:T(8,128)(2,1)} %bitcast.5), custom_call_target="tpu_custom_call" | custom-call | tf_op jit(solution)/shard_map/load/pallas_call | solution.py:79
  4.5 0.0 collective-permute-done.other_v
  4.5 0.0 copy-start
  4.5 0.0 copy-start.1
  4.6 1.8 %whole_slots.1 = (bf16[16,4096]{1,0:T(8,128)(2,1)S(1)}, bf16[16,4096]{1,0:T(8,128)(2,1)S(1)}, bf16[16,4096]{1,0:T(8,128)(2,1)S(1)}, bf16[16,4096]{1,0:T(8,128)(2,1)S(1)}, bf16[512,2048]{1,0:T(8,128)(2,1)}) custom-call(s32[8]{0:T(128)} %owner.1, s32[1]{0:T(128)} %bitcast.1.me, s32[1]{0:T(128)} %bitcast.core, ...), custom_call_target="tpu_custom_call", output_to_operand_aliasing={{4}: (7, {})} | custom-call | flops 67108864 | bytes 2097152 | tf_op jit(solution)/shard_map/whole_slots/pallas_call | solution.py:111
  6.4 0.1 collective-permute-start.9
  6.5 4.0 %collective-permute-start.1 = (bf16[16,4096]{1,0:T(8,128)(2,1)S(1)}, bf16[16,4096]{1,0:T(8,128)(2,1)S(1)}, u32[]{:S(2)}, u32[]{:S(2)}) collective-permute-start(bf16[16,4096]{1,0:T(8,128)(2,1)S(1)} %get-tuple-element.15), channel_id=1, source_target_pairs={{0,8},{1,11},{2,10},{3,9},{4,12},{5,15},{6,14},{7,13},{8,0},{9,3},... | collective-permute-start | bytes 393224 | tf_op jit(solution)/shard_map/ppermute | solution.py:237
  10.6 1.4 %collective-permute-start.2 = (bf16[16,4096]{1,0:T(8,128)(2,1)S(1)}, bf16[16,4096]{1,0:T(8,128)(2,1)S(1)}, u32[]{:S(2)}, u32[]{:S(2)}) collective-permute-start(bf16[16,4096]{1,0:T(8,128)(2,1)S(1)} %get-tuple-element.16), channel_id=1, source_target_pairs={{0,12},{1,15},{2,14},{3,13},{4,8},{5,11},{6,10},{7,9},{8,4},{9,7},... | collective-permute-start | bytes 393224 | tf_op jit(solution)/shard_map/ppermute | solution.py:237
  11.9 1.5 %collective-permute-start.3 = (bf16[16,4096]{1,0:T(8,128)(2,1)S(1)}, bf16[16,4096]{1,0:T(8,128)(2,1)S(1)}, u32[]{:S(2)}, u32[]{:S(2)}) collective-permute-start(bf16[16,4096]{1,0:T(8,128)(2,1)S(1)} %get-tuple-element.17), channel_id=1, source_target_pairs={{0,2},{1,5},{2,0},{3,7},{4,6},{5,1},{6,4},{7,3},{8,10},{9,13},{10,... | collective-permute-start | bytes 393224 | tf_op jit(solution)/shard_map/ppermute | solution.py:237
  13.4 2.1 %collective-permute-start.4 = (bf16[16,4096]{1,0:T(8,128)(2,1)S(1)}, bf16[16,4096]{1,0:T(8,128)(2,1)S(1)}, u32[]{:S(2)}, u32[]{:S(2)}) collective-permute-start(bf16[16,4096]{1,0:T(8,128)(2,1)S(1)} %get-tuple-element.18), channel_id=1, source_target_pairs={{0,6},{1,1},{2,4},{3,3},{4,2},{5,5},{6,0},{7,7},{8,14},{9,9},{10,1... | collective-permute-start | bytes 393224 | tf_op jit(solution)/shard_map/ppermute | solution.py:237
  15.5 4.8 %collective-permute-done.1.refs_0_ = bf16[16,4096]{1,0:T(8,128)(2,1)S(1)} collective-permute-done((bf16[16,4096]{1,0:T(8,128)(2,1)S(1)}, bf16[16,4096]{1,0:T(8,128)(2,1)S(1)}, u32[]{:S(2)}, u32[]{:S(2)}) %collective-permute-start.1) | collective-permute-done | bytes 131104 | tf_op jit(solution)/shard_map/ppermute | solution.py:237
  20.3 0.0 collective-permute-start.5
  20.3 0.0 collective-permute-done.2.refs_1_
  20.3 0.5 %collective-permute-start.6 = (bf16[16,4096]{1,0:T(8,128)(2,1)S(1)}, bf16[16,4096]{1,0:T(8,128)(2,1)S(1)}, u32[]{:S(2)}, u32[]{:S(2)}) collective-permute-start(bf16[16,4096]{1,0:T(8,128)(2,1)S(1)} %collective-permute-done.2.refs_1_), channel_id=1, source_target_pairs={{0,1},{1,0},{2,3},{3,2},{4,5},{5,4},{6,7},{7,6},{8,9},{9,8},{10,11... | collective-permute-start | bytes 393224 | tf_op jit(solution)/shard_map/ppermute | solution.py:243
  20.8 0.0 collective-permute-done.3.refs_2_
  20.8 0.1 collective-permute-start.7
  20.9 2.3 %collective-permute-done.4.refs_3_ = bf16[16,4096]{1,0:T(8,128)(2,1)S(1)} collective-permute-done((bf16[16,4096]{1,0:T(8,128)(2,1)S(1)}, bf16[16,4096]{1,0:T(8,128)(2,1)S(1)}, u32[]{:S(2)}, u32[]{:S(2)}) %collective-permute-start.4) | collective-permute-done | bytes 131104 | tf_op jit(solution)/shard_map/ppermute | solution.py:237
  23.2 0.0 collective-permute-start.8
  23.2 0.0 collective-permute-done.5.refs_4_
  23.2 0.0 collective-permute-done.6.refs_5_
  23.2 0.0 collective-permute-done.7.refs_6_
  23.2 1.3 %collective-permute-done.8.refs_7_ = bf16[16,4096]{1,0:T(8,128)(2,1)S(1)} collective-permute-done((bf16[16,4096]{1,0:T(8,128)(2,1)S(1)}, bf16[16,4096]{1,0:T(8,128)(2,1)S(1)}, u32[]{:S(2)}, u32[]{:S(2)}) %collective-permute-start.8) | collective-permute-done | bytes 131104 | tf_op jit(solution)/shard_map/ppermute | solution.py:243
  24.6 0.0 collective-permute-done.9.refs_9_
  24.6 0.0 copy-done
  24.6 0.0 copy-done.1
  24.6 2.3 %scores.1 = (f32[64,512]{1,0:T(8,128)}, bf16[128,4096]{1,0:T(8,128)(2,1)S(1)}) custom-call(s32[1]{0:T(128)} %bitcast.core, s32[1]{0:T(128)} %bitcast.1.me, s32[1,128]{1,0:T(1,128)S(1)} %bitcast.7, bf16[16,4096]{1,0:T(8,128)(2,1)S(1)} %collective-permute-done.1.refs_0_, bf16[16,4096]{1,0:T(8,128)(2,1)S(1)} %collective-permute-done.2.refs_1_, ...), custom_call_target="tpu_custom_call" | custom-call | flops 268435456 | bytes 5242880 | tf_op jit(solution)/shard_map/scores/pallas_call | solution.py:163
  26.9 5.3 %all-to-all-start = ((f32[8,8,512]{2,1,0:T(8,128)}), f32[8,8,512]{2,1,0:T(8,128)S(1)}, u32[]{:S(2)}, u32[]{:S(2)}) async-start(f32[8,8,512]{2,1,0:T(8,128)} %bitcast.4), calls=%async_computation | async-start | bytes 262144 | tf_op jit(solution)/shard_map/all_to_all | solution.py:245
  32.2 7.1 %fisher.1 = bf16[1,2048,4096]{2,1,0:T(8,128)(2,1)} custom-call(s32[1]{0:T(128)} %bitcast.core, bf16[128,4096]{1,0:T(8,128)(2,1)S(1)} %get-tuple-element.20.x_ref), custom_call_target="tpu_custom_call" | custom-call | flops 2147483648 | bytes 17825792 | tf_op jit(solution)/shard_map/fisher/pallas_call | solution.py:207
  39.3 0.4 all-to-all-done
  39.6 0.6 %reduce_sum.9 = f32[8,512]{1,0:T(8,128)} reduce(f32[8,8,512]{2,1,0:T(8,128)S(1)} %all-to-all-done, f32[]{:T(128)} %constant.9.clone.1), dimensions={0}, to_apply=%region_0.0 | reduce | flops 28672 | bytes 147460 | tf_op jit(solution)/shard_map/reduce_sum | solution.py:249
Async XLA Ops:
  0.6 3.9 %collective-permute-start = (bf16[16,8,32,128]{3,2,1,0:T(8,128)(2,1)}, bf16[16,8,32,128]{3,2,1,0:T(8,128)(2,1)S(1)}, u32[]{:S(2)}, u32[]{:S(2)}) collective-permute-start(bf16[16,8,32,128]{3,2,1,0:T(8,128)(2,1)} %refs_0_.1), channel_id=1, source_target_pairs={{0,1},{1,0},{2,3},{3,2},{4,5},{5,4},{6,7},{7,6},{8,9},{9,8},{10,11... | collective-permute-start | bytes 3145736 | tf_op jit(solution)/shard_map/ppermute | solution.py:230
  4.5 20.0 %copy-start = (bf16[1,512,2048]{2,1,0:T(8,128)(2,1)S(1)}, bf16[1,512,2048]{2,1,0:T(8,128)(2,1)}, u32[]{:S(2)}) copy-start(bf16[1,512,2048]{2,1,0:T(8,128)(2,1)} %param.11) | copy-start | bytes 6291460
  4.5 20.0 %copy-start.1 = (s32[128]{0:T(128)S(1)}, s32[128]{0:T(128)}, u32[]{:S(2)}) copy-start(s32[128]{0:T(128)} %param.9) | copy-start | bytes 1540
  6.4 18.1 %collective-permute-start.9 = (bf16[512,2048]{1,0:T(8,128)(2,1)}, bf16[512,2048]{1,0:T(8,128)(2,1)S(1)}, u32[]{:S(2)}, u32[]{:S(2)}) collective-permute-start(bf16[512,2048]{1,0:T(8,128)(2,1)} %get-tuple-element.19), channel_id=1, source_target_pairs={{0,1},{1,0},{2,3},{3,2},{4,5},{5,4},{6,7},{7,6},{8,9},{9,8},{10,11... | collective-permute-start | bytes 6291464 | tf_op jit(solution)/shard_map/ppermute | solution.py:242
  6.5 13.8 %collective-permute-start.1 = (bf16[16,4096]{1,0:T(8,128)(2,1)S(1)}, bf16[16,4096]{1,0:T(8,128)(2,1)S(1)}, u32[]{:S(2)}, u32[]{:S(2)}) collective-permute-start(bf16[16,4096]{1,0:T(8,128)(2,1)S(1)} %get-tuple-element.15), channel_id=1, source_target_pairs={{0,8},{1,11},{2,10},{3,9},{4,12},{5,15},{6,14},{7,13},{8,0},{9,3},... | collective-permute-start | bytes 393224 | tf_op jit(solution)/shard_map/ppermute | solution.py:237
  10.6 9.8 %collective-permute-start.2 = (bf16[16,4096]{1,0:T(8,128)(2,1)S(1)}, bf16[16,4096]{1,0:T(8,128)(2,1)S(1)}, u32[]{:S(2)}, u32[]{:S(2)}) collective-permute-start(bf16[16,4096]{1,0:T(8,128)(2,1)S(1)} %get-tuple-element.16), channel_id=1, source_target_pairs={{0,12},{1,15},{2,14},{3,13},{4,8},{5,11},{6,10},{7,9},{8,4},{9,7},... | collective-permute-start | bytes 393224 | tf_op jit(solution)/shard_map/ppermute | solution.py:237
  11.9 8.9 %collective-permute-start.3 = (bf16[16,4096]{1,0:T(8,128)(2,1)S(1)}, bf16[16,4096]{1,0:T(8,128)(2,1)S(1)}, u32[]{:S(2)}, u32[]{:S(2)}) collective-permute-start(bf16[16,4096]{1,0:T(8,128)(2,1)S(1)} %get-tuple-element.17), channel_id=1, source_target_pairs={{0,2},{1,5},{2,0},{3,7},{4,6},{5,1},{6,4},{7,3},{8,10},{9,13},{10,... | collective-permute-start | bytes 393224 | tf_op jit(solution)/shard_map/ppermute | solution.py:237
  13.4 9.8 %collective-permute-start.4 = (bf16[16,4096]{1,0:T(8,128)(2,1)S(1)}, bf16[16,4096]{1,0:T(8,128)(2,1)S(1)}, u32[]{:S(2)}, u32[]{:S(2)}) collective-permute-start(bf16[16,4096]{1,0:T(8,128)(2,1)S(1)} %get-tuple-element.18), channel_id=1, source_target_pairs={{0,6},{1,1},{2,4},{3,3},{4,2},{5,5},{6,0},{7,7},{8,14},{9,9},{10,1... | collective-permute-start | bytes 393224 | tf_op jit(solution)/shard_map/ppermute | solution.py:237
  20.3 2.9 %collective-permute-start.5 = (bf16[16,4096]{1,0:T(8,128)(2,1)S(1)}, bf16[16,4096]{1,0:T(8,128)(2,1)S(1)}, u32[]{:S(2)}, u32[]{:S(2)}) collective-permute-start(bf16[16,4096]{1,0:T(8,128)(2,1)S(1)} %collective-permute-done.1.refs_0_), channel_id=1, source_target_pairs={{0,1},{1,0},{2,3},{3,2},{4,5},{5,4},{6,7},{7,6},{8,9},{9,8},{10,11... | collective-permute-start | bytes 393224 | tf_op jit(solution)/shard_map/ppermute | solution.py:243
  20.3 2.9 %collective-permute-start.6 = (bf16[16,4096]{1,0:T(8,128)(2,1)S(1)}, bf16[16,4096]{1,0:T(8,128)(2,1)S(1)}, u32[]{:S(2)}, u32[]{:S(2)}) collective-permute-start(bf16[16,4096]{1,0:T(8,128)(2,1)S(1)} %collective-permute-done.2.refs_1_), channel_id=1, source_target_pairs={{0,1},{1,0},{2,3},{3,2},{4,5},{5,4},{6,7},{7,6},{8,9},{9,8},{10,11... | collective-permute-start | bytes 393224 | tf_op jit(solution)/shard_map/ppermute | solution.py:243
  20.8 2.4 %collective-permute-start.7 = (bf16[16,4096]{1,0:T(8,128)(2,1)S(1)}, bf16[16,4096]{1,0:T(8,128)(2,1)S(1)}, u32[]{:S(2)}, u32[]{:S(2)}) collective-permute-start(bf16[16,4096]{1,0:T(8,128)(2,1)S(1)} %collective-permute-done.3.refs_2_), channel_id=1, source_target_pairs={{0,1},{1,0},{2,3},{3,2},{4,5},{5,4},{6,7},{7,6},{8,9},{9,8},{10,11... | collective-permute-start | bytes 393224 | tf_op jit(solution)/shard_map/ppermute | solution.py:243
  23.2 1.3 %collective-permute-start.8 = (bf16[16,4096]{1,0:T(8,128)(2,1)S(1)}, bf16[16,4096]{1,0:T(8,128)(2,1)S(1)}, u32[]{:S(2)}, u32[]{:S(2)}) collective-permute-start(bf16[16,4096]{1,0:T(8,128)(2,1)S(1)} %collective-permute-done.4.refs_3_), channel_id=1, source_target_pairs={{0,1},{1,0},{2,3},{3,2},{4,5},{5,4},{6,7},{7,6},{8,9},{9,8},{10,11... | collective-permute-start | bytes 393224 | tf_op jit(solution)/shard_map/ppermute | solution.py:243
  26.9 12.8 %all-to-all-start = ((f32[8,8,512]{2,1,0:T(8,128)}), f32[8,8,512]{2,1,0:T(8,128)S(1)}, u32[]{:S(2)}, u32[]{:S(2)}) async-start(f32[8,8,512]{2,1,0:T(8,128)} %bitcast.4), calls=%async_computation | async-start | bytes 262144 | tf_op jit(solution)/shard_map/all_to_all | solution.py:245

commit v3 on v2

v3 whole, which is shorter than its diff:
```python
import functools

import jax
import jax.numpy as jnp
from jax import lax
from jax.experimental import pallas as pl
from jax.experimental.pallas import tpu as pltpu
from jax.sharding import PartitionSpec as P

NT = (((1,), (1,)), ((), ()))
TN = (((0,), (0,)), ((), ()))
VMEM = pl.BlockSpec(memory_space=pltpu.VMEM)
SMEM = pl.BlockSpec(memory_space=pltpu.SMEM)
HBM = pl.BlockSpec(memory_space=pl.ANY)


def here(x):
    return pltpu.with_memory_space_constraint(x, pltpu.VMEM)


def scalars(x):
    return pltpu.with_memory_space_constraint(x, pltpu.SMEM)


def far(x):
    return pltpu.with_memory_space_constraint(x, pltpu.HBM)


def matrix_at(owner, slot):
    matrix = jnp.int32(0)
    for m in range(owner.shape[0]):
        matrix = jnp.where(owner[m] == slot, m, matrix)
    return matrix


def slot_rows(in_v, other_v, out_v, matrix, length_of, tiles, store):
    seqs, _, width, length = out_v.shape
    rows = 2 * in_v.shape[2]
    stride = tiles.shape[0] // seqs
    per = length // width
    scale = length ** (-0.5)
    lane = lax.broadcasted_iota(jnp.int32, (1, length), 1)
    for s in range(seqs):
        left = jnp.concatenate([in_v[s, matrix], other_v[s, matrix]], axis=0)
        left = jnp.where(lane < length_of(s), left, 0)
        tile = lax.dot_general(left, out_v[s, matrix], NT, preferred_element_type=jnp.float32)
        tiles[s * stride:s * stride + rows, :] = jnp.concatenate([tile] * per, axis=1)
    for t in range(rows // per):
        tile = tiles[pl.ds(per * t, seqs, stride=stride), :]
        for p in range(1, per):
            other = tiles[pl.ds(per * t + p, seqs, stride=stride), :]
            tile = jnp.where(lane < p * width, tile, other)
        store(t * length, (tile * scale).astype(jnp.bfloat16))


def load_body(pairs, owner_hbm, lengths_hbm, *refs):
    *refs, facts, owner, lengths, sem, small = refs
    n = len(refs) // 2
    parts = sem.shape[1]
    copies = []
    for i in range(n):
        each = refs[i].shape[0] // parts
        for j in range(parts):
            part = pl.ds(j * each, each)
            copies.append(pltpu.make_async_copy(refs[i].at[part], refs[n + i].at[part], sem.at[i, j]))
    scalar_copies = [
        pltpu.make_async_copy(owner_hbm, owner, small.at[0]),
        pltpu.make_async_copy(lengths_hbm, lengths, small.at[1]),
    ]
    for copy in scalar_copies + copies:
        copy.start()
    core, me = lax.axis_index("mat"), lax.axis_index("dp")
    facts[0] = core
    facts[1] = me
    for copy in scalar_copies:
        copy.wait()
    for at, pair in enumerate(pairs):
        facts[2 + at] = matrix_at(owner, me ^ jnp.where(core == 0, pair[0], pair[1]))
    for s in range(lengths.shape[0]):
        facts[2 + len(pairs) + s] = lengths[s]
    for copy in copies:
        copy.wait()


def load(pairs, owner, lengths, *arrays):
    parts = 4 if all(a.shape[0] % 4 == 0 for a in arrays) else 1
    return pl.pallas_call(
        functools.partial(load_body, pairs),
        out_shape=[pltpu.VMEM(a.shape, a.dtype) for a in arrays]
        + [pltpu.SMEM((2 + len(pairs) + lengths.shape[0],), jnp.int32)],
        in_specs=[HBM] * (2 + len(arrays)),
        out_specs=[VMEM] * len(arrays) + [SMEM],
        scratch_shapes=[
            pltpu.SMEM(owner.shape, jnp.int32),
            pltpu.SMEM(lengths.shape, jnp.int32),
            pltpu.SemaphoreType.DMA((len(arrays), parts)),
            pltpu.SemaphoreType.DMA((2,)),
        ],
        compiler_params=pltpu.CompilerParams(vmem_limit_bytes=4 << 20),
        name="load",
    )(far(owner), far(lengths), *[far(a) for a in arrays])


def whole_body(n, facts, in_v, other_v, out_v, _, *refs):
    grads, tiles = refs[:n], refs[-1]
    half = grads[0].shape[1] // 2
    for at in range(n):

        def store(column, x):
            first = jnp.where(facts[0] == 0, column, (column + half) % (2 * half))
            grads[at][:, pl.ds(pl.multiple_of(first, 128), x.shape[1])] = x

        slot_rows(in_v, other_v, out_v, facts[2 + at], lambda s: facts[2 + n + s], tiles.at[at % 2], store)


def whole_slots(n, facts, in_v, other_in, out_v, passed):
    seqs, _, rows, length = in_v.shape
    width = out_v.shape[2]
    return pl.pallas_call(
        functools.partial(whole_body, n),
        out_shape=[pltpu.VMEM((seqs, 2 * rows * width), jnp.bfloat16)] * n
        + [pltpu.VMEM(passed.shape, passed.dtype)],
        in_specs=[SMEM] + [VMEM] * 4,
        out_specs=[VMEM] * (n + 1),
        input_output_aliases={4: n},
        scratch_shapes=[pltpu.VMEM((2, seqs * (2 * rows + 8), length), jnp.float32)],
        compiler_params=pltpu.CompilerParams(vmem_limit_bytes=12 << 20),
        cost_estimate=pl.CostEstimate(
            flops=4 * n * seqs * rows * width * length,
            bytes_accessed=2 * n * seqs * length * (2 * rows + width),
            transcendentals=0,
        ),
        name="whole_slots",
    )(scalars(facts), here(in_v), here(other_in), here(out_v), here(passed))


def score_body(pairs, rows_each, cores, facts, ids, *refs):
    core, me = facts[0], facts[1]
    mine, theirs = refs[:len(pairs)], refs[len(pairs):2 * len(pairs)]
    own_q, other_q, s_ref, x_ref = refs[2 * len(pairs):]
    seqs, width = mine[0].shape
    half = width // 2
    rows = s_ref.shape[0]
    total = ids.shape[1]
    own_at = pl.ds(pl.multiple_of(core * half, 128), half)
    other_at = pl.ds(pl.multiple_of((1 - core) * half, 128), half)

    def place(k):
        return pl.ds(pl.multiple_of((me ^ k) * seqs, 16), seqs)

    for pair, own, other in zip(pairs, mine, theirs):
        x_ref[place(jnp.where(core == 0, pair[0], pair[1])), :] = own[...]
        x_ref[place(jnp.where(core == 0, pair[1], pair[0])), :] = other[...]
    at = lax.broadcasted_iota(jnp.int32, (rows, total), 0)
    wanted = (at // rows_each * cores + core) * rows_each + at % rows_each
    pick = jnp.where(wanted == ids[...], 1.0, 0.0).astype(jnp.bfloat16)
    for first, where, q_ref in ((True, own_at, own_q), (False, other_at, other_q)):
        picked = jnp.dot(pick, x_ref[:, where], preferred_element_type=jnp.float32).astype(jnp.bfloat16)
        part = lax.dot_general(picked, q_ref[...], NT, preferred_element_type=jnp.float32)
        s_ref[...] = part if first else s_ref[...] + part


def partial_scores(pairs, facts, ids, mine, theirs, own_q, other_q):
    cores = 2
    seqs, width = mine[0].shape
    half = width // 2
    total = ids.shape[1]
    queries = own_q.shape[0]
    rows = total // cores
    rows_each = rows // (total // seqs)
    args = [*mine, *theirs, own_q, other_q]
    return pl.pallas_call(
        functools.partial(score_body, pairs, rows_each, cores),
        out_shape=[pltpu.VMEM((rows, queries), jnp.float32), pltpu.VMEM((total, 2 * half), jnp.bfloat16)],
        in_specs=[SMEM] + [VMEM] * (1 + len(args)),
        out_specs=[VMEM] * 2,
        compiler_params=pltpu.CompilerParams(vmem_limit_bytes=16 << 20),
        cost_estimate=pl.CostEstimate(
            flops=4 * rows * queries * half, bytes_accessed=4 * half * (queries + total), transcendentals=0
        ),
        name="scores",
    )(scalars(facts), ids, *[here(arg) for arg in args])


def fisher_body(total, facts, x_ref, f_hbm, left, out, sem):
    half = x_ref.shape[1] // 2
    depth, block, _ = out.shape
    step = 512 if half % 512 == 0 else half
    for at in range(0, half, block):
        where = pl.ds(pl.multiple_of(facts[0] * half + at, 128), block)
        left[at:at + block, :] = x_ref[:, where].T

    def copy(i):
        rows = pl.ds(pl.multiple_of(i * block, block), block)
        return pltpu.make_async_copy(out.at[i % depth], f_hbm.at[0, rows], sem.at[i % depth])

    @pl.loop(0, half // block)
    def _(i):
        @pl.when(i >= depth)
        def _():
            copy(i - depth).wait()

        rows = left[pl.ds(pl.multiple_of(i * block, block), block), :]
        for at in range(0, 2 * half, step):
            tile = jnp.dot(rows, x_ref[:, at:at + step], preferred_element_type=jnp.float32)
            out[i % depth, :, at:at + step] = (tile * (1.0 / total)).astype(out.dtype)
        copy(i).start()

    for i in range(half // block - depth, half // block):
        copy(i).wait()


def fisher_block(facts, x):
    total, half = x.shape[0], x.shape[1] // 2
    block, depth = (256, 4) if half % 256 == 0 and half >= 1024 else (half, 1)
    return pl.pallas_call(
        functools.partial(fisher_body, total),
        out_shape=jax.ShapeDtypeStruct((1, half, 2 * half), jnp.bfloat16),
        in_specs=[SMEM, VMEM],
        out_specs=HBM,
        scratch_shapes=[
            pltpu.VMEM((half, total), jnp.bfloat16),
            pltpu.VMEM((depth, block, 2 * half), jnp.bfloat16),
            pltpu.SemaphoreType.DMA((depth,)),
        ],
        compiler_params=pltpu.CompilerParams(vmem_limit_bytes=24 << 20),
        cost_estimate=pl.CostEstimate(
            flops=4 * total * half * half, bytes_accessed=4 * half * (half + total), transcendentals=0
        ),
        name="fisher",
    )(scalars(facts), here(x))


def local(dp, cores, in_factor, out_factor, seq_lengths, sequence_ids, matrix_owner, queries):
    assert cores == 2 and dp % 2 == 0 and dp & (dp - 1) == 0
    swap = [(0, 1), (1, 0)]
    order = list(range(dp // 2, dp)) + list(range(1, dp // 2)) + [0]
    pairs = tuple(zip(order[::2], order[1::2]))
    other_in = lax.ppermute(in_factor, "mat", swap)
    in_v, out_v, own_q, facts = load(
        pairs, matrix_owner, seq_lengths, in_factor, out_factor, queries[0]
    )
    *made, own_q = whole_slots(len(pairs), facts, in_v, other_in, out_v, own_q)
    mine = [
        lax.ppermute(
            piece, ("dp", "mat"), [(d * 2 + c, (d ^ pair[c]) * 2 + c) for d in range(dp) for c in range(2)]
        )
        for pair, piece in zip(pairs, made)
    ]
    other_q = lax.ppermute(own_q, "mat", swap)
    theirs = [lax.ppermute(piece, "mat", swap) for piece in mine]
    part, x = partial_scores(pairs, facts, sequence_ids[None, :], mine, theirs, own_q, other_q)
    parts = lax.all_to_all(
        part.reshape(dp, part.shape[0] // dp, -1), "dp", split_axis=0, concat_axis=0, tiled=True
    )
    fisher = fisher_block(facts, x)
    return (fisher, jnp.sum(parts, axis=0))


def solution(mesh):
    in_specs = (
        P(("groups", "dp"), None, "mat", None),
        P(("groups", "dp"), None, None, None),
        P(("groups", "dp")),
        P("groups"),
        P(),
        P("dp", None, "mat"),
    )
    out_specs = (P(("groups", "dp"), "mat", None), P(("groups", "dp", "mat"), None))
    body = functools.partial(local, mesh.shape["dp"], mesh.shape["mat"])
    return jax.shard_map(body, mesh=mesh, in_specs=in_specs, out_specs=out_specs, check_vma=False)
```

time: 40.5 us -> 38.9 us (0.960)
  Pallas kernels: 14.6 us -> 13 us
    pallas_call x2, Pallas kernels: 5.21 us -> 3.61 us  [the longest x1 2.59 us: load(): pl.pallas_call(functools.partial(load_body, pairs), out_shape=[pltpu.VMEM...]
  transfers between devices with their start and end apart: 11 -> 11, of which waited for: 4 -> 4; matrix products, arithmetic and copies ran while one was open for 0% -> 0% of each run, Pallas kernels for 26% -> 25%
where the time goes in v3:
time: 38.9 us; the launch traced here: 38.6 us
  starting transfers between devices  15.4 us (40%)
  Pallas kernels  13 us (33%)
  waiting for transfers between devices  8.93 us (23%)
  between operations  0.7 us (2%)
  other arithmetic  0.62 us (2%)
    ppermute x4, starting transfers between devices, local(): lax.ppermute(piece, ('dp', 'mat'), [(d * 2 + c, (d ^ pair[c]) * 2 + c) fo...  8.78 us
    ppermute x4, waiting for transfers between devices, local(): lax.ppermute(piece, ('dp', 'mat'), [(d * 2 + c, (d ^ pair[c]) * 2 + c) fo...  7.24 us
    pallas_call x1, Pallas kernels, fisher_block(): pl.pallas_call(functools.partial(fisher_body, total), out_shape=jax.Shape...  7.11 us
    all_to_all x1, starting transfers between devices, local(): lax.all_to_all(part.reshape(dp, part.shape[0] // dp, -1), 'dp', split_axi...  5.14 us
    pallas_call x1, Pallas kernels, load(): pl.pallas_call(functools.partial(load_body, pairs), out_shape=[pltpu.VMEM...  2.59 us
    pallas_call x1, Pallas kernels, partial_scores(): pl.pallas_call(functools.partial(score_body, pairs, rows_each, cores), ou...  2.32 us
    ppermute x4, waiting for transfers between devices, local(): theirs = [lax.ppermute(piece, 'mat', swap) for piece in mine]  1.33 us
    pallas_call x1, Pallas kernels, whole_slots(): pl.pallas_call(functools.partial(whole_body, n), out_shape=[pltpu.VMEM((s...  1.03 us
  transfers between devices with their start and end apart: 11, of which 4 were waited for; matrix products, arithmetic and copies ran while one was open for 0% of the time, Pallas kernels for 25%

profile of v3, /device:TPU:0, one launch (start us, length us, event | category | flops | bytes accessed | tf_op | source)
XLA Modules:
  0.0 38.6 jit_solution(13495856774109825248)
XLA Ops:
  0.6 0.5 %collective-permute-start = (bf16[16,8,32,128]{3,2,1,0:T(8,128)(2,1)}, bf16[16,8,32,128]{3,2,1,0:T(8,128)(2,1)S(1)}, u32[]{:S(2)}, u32[]{:S(2)}) collective-permute-start(bf16[16,8,32,128]{3,2,1,0:T(8,128)(2,1)} %refs_0_.1), channel_id=1, source_target_pairs={{0,1},{1,0},{2,3},{3,2},{4,5},{5,4},{6,7},{7,6},{8,9},{9,8},{10,11... | collective-permute-start | bytes 3145736 | tf_op jit(solution)/shard_map/ppermute | solution.py:239
  1.1 2.6 %load.1 = (bf16[16,8,32,128]{3,2,1,0:T(8,128)(2,1)S(1)}, bf16[16,8,64,128]{3,2,1,0:T(8,128)(2,1)S(1)}, bf16[512,2048]{1,0:T(8,128)(2,1)S(1)}, s32[22]{0:T(128)S(4)}) custom-call(s32[8]{0:T(128)} %owner_hbm.1, s32[16]{0:T(128)} %lengths_hbm.1, bf16[16,8,32,128]{3,2,1,0:T(8,128)(2,1)} %refs_0_.1, bf16[16,8,64,128]{3,2,1,0:T(8,128)(2,1)} %refs_1_.1, ...), custom_call_target="tpu_custom_call" | custom-call | tf_op jit(solution)/shard_map/load/pallas_call | solution.py:87
  3.7 0.0 collective-permute-done.other_v
  3.8 0.0 copy-start
  3.8 1.0 %whole_slots.1 = (bf16[16,4096]{1,0:T(8,128)(2,1)S(1)}, bf16[16,4096]{1,0:T(8,128)(2,1)S(1)}, bf16[16,4096]{1,0:T(8,128)(2,1)S(1)}, bf16[16,4096]{1,0:T(8,128)(2,1)S(1)}, bf16[512,2048]{1,0:T(8,128)(2,1)S(1)}) custom-call(s32[22]{0:T(128)S(4)} %get-tuple-element.13.facts, ...), custom_call_target="tpu_custom_call", output_to_operand_aliasing={{4}: (4, {})} | custom-call | flops 67108864 | bytes 2097152 | tf_op jit(solution)/shard_map/whole_slots/pallas_call | solution.py:119
  4.8 0.3 collective-permute-start.9
  5.1 3.9 %collective-permute-start.1 = (bf16[16,4096]{1,0:T(8,128)(2,1)S(1)}, bf16[16,4096]{1,0:T(8,128)(2,1)S(1)}, u32[]{:S(2)}, u32[]{:S(2)}) collective-permute-start(bf16[16,4096]{1,0:T(8,128)(2,1)S(1)} %get-tuple-element.17), channel_id=1, source_target_pairs={{0,8},{1,11},{2,10},{3,9},{4,12},{5,15},{6,14},{7,13},{8,0},{9,3},... | collective-permute-start | bytes 393224 | tf_op jit(solution)/shard_map/ppermute | solution.py:245
  9.0 1.3 %collective-permute-start.2 = (bf16[16,4096]{1,0:T(8,128)(2,1)S(1)}, bf16[16,4096]{1,0:T(8,128)(2,1)S(1)}, u32[]{:S(2)}, u32[]{:S(2)}) collective-permute-start(bf16[16,4096]{1,0:T(8,128)(2,1)S(1)} %get-tuple-element.18), channel_id=1, source_target_pairs={{0,12},{1,15},{2,14},{3,13},{4,8},{5,11},{6,10},{7,9},{8,4},{9,7},... | collective-permute-start | bytes 393224 | tf_op jit(solution)/shard_map/ppermute | solution.py:245
  10.3 1.5 %collective-permute-start.3 = (bf16[16,4096]{1,0:T(8,128)(2,1)S(1)}, bf16[16,4096]{1,0:T(8,128)(2,1)S(1)}, u32[]{:S(2)}, u32[]{:S(2)}) collective-permute-start(bf16[16,4096]{1,0:T(8,128)(2,1)S(1)} %get-tuple-element.19), channel_id=1, source_target_pairs={{0,2},{1,5},{2,0},{3,7},{4,6},{5,1},{6,4},{7,3},{8,10},{9,13},{10,... | collective-permute-start | bytes 393224 | tf_op jit(solution)/shard_map/ppermute | solution.py:245
  11.8 2.1 %collective-permute-start.4 = (bf16[16,4096]{1,0:T(8,128)(2,1)S(1)}, bf16[16,4096]{1,0:T(8,128)(2,1)S(1)}, u32[]{:S(2)}, u32[]{:S(2)}) collective-permute-start(bf16[16,4096]{1,0:T(8,128)(2,1)S(1)} %get-tuple-element.20), channel_id=1, source_target_pairs={{0,6},{1,1},{2,4},{3,3},{4,2},{5,5},{6,0},{7,7},{8,14},{9,9},{10,1... | collective-permute-start | bytes 393224 | tf_op jit(solution)/shard_map/ppermute | solution.py:245
  13.9 4.6 %collective-permute-done.1.refs_0_ = bf16[16,4096]{1,0:T(8,128)(2,1)S(1)} collective-permute-done((bf16[16,4096]{1,0:T(8,128)(2,1)S(1)}, bf16[16,4096]{1,0:T(8,128)(2,1)S(1)}, u32[]{:S(2)}, u32[]{:S(2)}) %collective-permute-start.1) | collective-permute-done | bytes 131104 | tf_op jit(solution)/shard_map/ppermute | solution.py:245
  18.5 0.1 collective-permute-start.5
  18.6 0.0 collective-permute-done.2.refs_1_
  18.6 0.4 %collective-permute-start.6 = (bf16[16,4096]{1,0:T(8,128)(2,1)S(1)}, bf16[16,4096]{1,0:T(8,128)(2,1)S(1)}, u32[]{:S(2)}, u32[]{:S(2)}) collective-permute-start(bf16[16,4096]{1,0:T(8,128)(2,1)S(1)} %collective-permute-done.2.refs_1_), channel_id=1, source_target_pairs={{0,1},{1,0},{2,3},{3,2},{4,5},{5,4},{6,7},{7,6},{8,9},{9,8},{10,11... | collective-permute-start | bytes 393224 | tf_op jit(solution)/shard_map/ppermute | solution.py:251
  19.0 0.0 collective-permute-done.3.refs_2_
  19.0 0.1 collective-permute-start.7
  19.1 2.6 %collective-permute-done.4.refs_3_ = bf16[16,4096]{1,0:T(8,128)(2,1)S(1)} collective-permute-done((bf16[16,4096]{1,0:T(8,128)(2,1)S(1)}, bf16[16,4096]{1,0:T(8,128)(2,1)S(1)}, u32[]{:S(2)}, u32[]{:S(2)}) %collective-permute-start.4) | collective-permute-done | bytes 131104 | tf_op jit(solution)/shard_map/ppermute | solution.py:245
  21.8 0.0 collective-permute-start.8
  21.8 0.0 collective-permute-done.5.refs_4_
  21.8 0.0 collective-permute-done.6.refs_5_
  21.8 0.0 collective-permute-done.7.refs_6_
  21.8 1.3 %collective-permute-done.8.refs_7_ = bf16[16,4096]{1,0:T(8,128)(2,1)S(1)} collective-permute-done((bf16[16,4096]{1,0:T(8,128)(2,1)S(1)}, bf16[16,4096]{1,0:T(8,128)(2,1)S(1)}, u32[]{:S(2)}, u32[]{:S(2)}) %collective-permute-start.8) | collective-permute-done | bytes 131104 | tf_op jit(solution)/shard_map/ppermute | solution.py:251
  23.1 0.0 collective-permute-done.9.refs_9_
  23.1 0.0 copy-done
  23.1 2.3 %scores.1 = (f32[64,512]{1,0:T(8,128)}, bf16[128,4096]{1,0:T(8,128)(2,1)S(1)}) custom-call(s32[22]{0:T(128)S(4)} %get-tuple-element.13.facts, s32[1,128]{1,0:T(1,128)S(1)} %bitcast.3, bf16[16,4096]{1,0:T(8,128)(2,1)S(1)} %collective-permute-done.1.refs_0_, bf16[16,4096]{1,0:T(8,128)(2,1)S(1)} %collective-permute-done.2.refs_1_, ...), custom_call_target="tpu_custom_call" | custom-call | flops 268435456 | bytes 5242880 | tf_op jit(solution)/shard_map/scores/pallas_call | solution.py:172
  25.4 5.1 %all-to-all-start = ((f32[8,8,512]{2,1,0:T(8,128)}), f32[8,8,512]{2,1,0:T(8,128)S(1)}, u32[]{:S(2)}, u32[]{:S(2)}) async-start(f32[8,8,512]{2,1,0:T(8,128)} %bitcast.2), calls=%async_computation | async-start | bytes 262144 | tf_op jit(solution)/shard_map/all_to_all | solution.py:253
  30.6 7.1 %fisher.1 = bf16[1,2048,4096]{2,1,0:T(8,128)(2,1)} custom-call(s32[22]{0:T(128)S(4)} %get-tuple-element.13.facts, bf16[128,4096]{1,0:T(8,128)(2,1)S(1)} %get-tuple-element.22.x_ref), custom_call_target="tpu_custom_call" | custom-call | flops 2147483648 | bytes 17825792 | tf_op jit(solution)/shard_map/fisher/pallas_call | solution.py:216
  37.7 0.4 all-to-all-done
  38.0 0.6 %reduce_sum.9 = f32[8,512]{1,0:T(8,128)} reduce(f32[8,8,512]{2,1,0:T(8,128)S(1)} %all-to-all-done, f32[]{:T(128)} %constant.0.clone.1), dimensions={0}, to_apply=%region_0.0 | reduce | flops 28672 | bytes 147460 | tf_op jit(solution)/shard_map/reduce_sum | solution.py:257
Async XLA Ops:
  0.6 3.1 %collective-permute-start = (bf16[16,8,32,128]{3,2,1,0:T(8,128)(2,1)}, bf16[16,8,32,128]{3,2,1,0:T(8,128)(2,1)S(1)}, u32[]{:S(2)}, u32[]{:S(2)}) collective-permute-start(bf16[16,8,32,128]{3,2,1,0:T(8,128)(2,1)} %refs_0_.1), channel_id=1, source_target_pairs={{0,1},{1,0},{2,3},{3,2},{4,5},{5,4},{6,7},{7,6},{8,9},{9,8},{10,11... | collective-permute-start | bytes 3145736 | tf_op jit(solution)/shard_map/ppermute | solution.py:239
  3.8 19.4 %copy-start = (s32[128]{0:T(128)S(1)}, s32[128]{0:T(128)}, u32[]{:S(2)}) copy-start(s32[128]{0:T(128)} %param.9) | copy-start | bytes 1540
  4.8 18.3 %collective-permute-start.9 = (bf16[512,2048]{1,0:T(8,128)(2,1)S(1)}, bf16[512,2048]{1,0:T(8,128)(2,1)S(1)}, u32[]{:S(2)}, u32[]{:S(2)}) collective-permute-start(bf16[512,2048]{1,0:T(8,128)(2,1)S(1)} %get-tuple-element.21.refs_8_), channel_id=1, source_target_pairs={{0,1},{1,0},{2,3},{3,2},{4,5},{5,4},{6,7},{7,6},{8,9},{9,8},{10,11... | collective-permute-start | bytes 6291464 | tf_op jit(solution)/shard_map/ppermute | solution.py:250
  5.1 13.4 %collective-permute-start.1 = (bf16[16,4096]{1,0:T(8,128)(2,1)S(1)}, bf16[16,4096]{1,0:T(8,128)(2,1)S(1)}, u32[]{:S(2)}, u32[]{:S(2)}) collective-permute-start(bf16[16,4096]{1,0:T(8,128)(2,1)S(1)} %get-tuple-element.17), channel_id=1, source_target_pairs={{0,8},{1,11},{2,10},{3,9},{4,12},{5,15},{6,14},{7,13},{8,0},{9,3},... | collective-permute-start | bytes 393224 | tf_op jit(solution)/shard_map/ppermute | solution.py:245
  9.0 9.7 %collective-permute-start.2 = (bf16[16,4096]{1,0:T(8,128)(2,1)S(1)}, bf16[16,4096]{1,0:T(8,128)(2,1)S(1)}, u32[]{:S(2)}, u32[]{:S(2)}) collective-permute-start(bf16[16,4096]{1,0:T(8,128)(2,1)S(1)} %get-tuple-element.18), channel_id=1, source_target_pairs={{0,12},{1,15},{2,14},{3,13},{4,8},{5,11},{6,10},{7,9},{8,4},{9,7},... | collective-permute-start | bytes 393224 | tf_op jit(solution)/shard_map/ppermute | solution.py:245
  10.3 8.7 %collective-permute-start.3 = (bf16[16,4096]{1,0:T(8,128)(2,1)S(1)}, bf16[16,4096]{1,0:T(8,128)(2,1)S(1)}, u32[]{:S(2)}, u32[]{:S(2)}) collective-permute-start(bf16[16,4096]{1,0:T(8,128)(2,1)S(1)} %get-tuple-element.19), channel_id=1, source_target_pairs={{0,2},{1,5},{2,0},{3,7},{4,6},{5,1},{6,4},{7,3},{8,10},{9,13},{10,... | collective-permute-start | bytes 393224 | tf_op jit(solution)/shard_map/ppermute | solution.py:245
  11.8 9.9 %collective-permute-start.4 = (bf16[16,4096]{1,0:T(8,128)(2,1)S(1)}, bf16[16,4096]{1,0:T(8,128)(2,1)S(1)}, u32[]{:S(2)}, u32[]{:S(2)}) collective-permute-start(bf16[16,4096]{1,0:T(8,128)(2,1)S(1)} %get-tuple-element.20), channel_id=1, source_target_pairs={{0,6},{1,1},{2,4},{3,3},{4,2},{5,5},{6,0},{7,7},{8,14},{9,9},{10,1... | collective-permute-start | bytes 393224 | tf_op jit(solution)/shard_map/ppermute | solution.py:245
  18.5 3.2 %collective-permute-start.5 = (bf16[16,4096]{1,0:T(8,128)(2,1)S(1)}, bf16[16,4096]{1,0:T(8,128)(2,1)S(1)}, u32[]{:S(2)}, u32[]{:S(2)}) collective-permute-start(bf16[16,4096]{1,0:T(8,128)(2,1)S(1)} %collective-permute-done.1.refs_0_), channel_id=1, source_target_pairs={{0,1},{1,0},{2,3},{3,2},{4,5},{5,4},{6,7},{7,6},{8,9},{9,8},{10,11... | collective-permute-start | bytes 393224 | tf_op jit(solution)/shard_map/ppermute | solution.py:251
  18.6 3.1 %collective-permute-start.6 = (bf16[16,4096]{1,0:T(8,128)(2,1)S(1)}, bf16[16,4096]{1,0:T(8,128)(2,1)S(1)}, u32[]{:S(2)}, u32[]{:S(2)}) collective-permute-start(bf16[16,4096]{1,0:T(8,128)(2,1)S(1)} %collective-permute-done.2.refs_1_), channel_id=1, source_target_pairs={{0,1},{1,0},{2,3},{3,2},{4,5},{5,4},{6,7},{7,6},{8,9},{9,8},{10,11... | collective-permute-start | bytes 393224 | tf_op jit(solution)/shard_map/ppermute | solution.py:251
  19.0 2.7 %collective-permute-start.7 = (bf16[16,4096]{1,0:T(8,128)(2,1)S(1)}, bf16[16,4096]{1,0:T(8,128)(2,1)S(1)}, u32[]{:S(2)}, u32[]{:S(2)}) collective-permute-start(bf16[16,4096]{1,0:T(8,128)(2,1)S(1)} %collective-permute-done.3.refs_2_), channel_id=1, source_target_pairs={{0,1},{1,0},{2,3},{3,2},{4,5},{5,4},{6,7},{7,6},{8,9},{9,8},{10,11... | collective-permute-start | bytes 393224 | tf_op jit(solution)/shard_map/ppermute | solution.py:251
  21.8 1.3 %collective-permute-start.8 = (bf16[16,4096]{1,0:T(8,128)(2,1)S(1)}, bf16[16,4096]{1,0:T(8,128)(2,1)S(1)}, u32[]{:S(2)}, u32[]{:S(2)}) collective-permute-start(bf16[16,4096]{1,0:T(8,128)(2,1)S(1)} %collective-permute-done.4.refs_3_), channel_id=1, source_target_pairs={{0,1},{1,0},{2,3},{3,2},{4,5},{5,4},{6,7},{7,6},{8,9},{9,8},{10,11... | collective-permute-start | bytes 393224 | tf_op jit(solution)/shard_map/ppermute | solution.py:251
  25.4 12.6 %all-to-all-start = ((f32[8,8,512]{2,1,0:T(8,128)}), f32[8,8,512]{2,1,0:T(8,128)S(1)}, u32[]{:S(2)}, u32[]{:S(2)}) async-start(f32[8,8,512]{2,1,0:T(8,128)} %bitcast.2), calls=%async_computation | async-start | bytes 262144 | tf_op jit(solution)/shard_map/all_to_all | solution.py:253

commit v4 on v3

--- a/solution.py
+++ b/solution.py
@@ -134,55 +134,53 @@
     )(scalars(facts), here(in_v), here(other_in), here(out_v), here(passed))
 
 
-def score_body(pairs, rows_each, cores, facts, ids, *refs):
+def score_body(pairs, facts, ids, *refs):
+    n = len(pairs)
+    pieces, (own_q, other_q, s_ref, x, t) = refs[:n], refs[n:]
     core, me = facts[0], facts[1]
-    mine, theirs = refs[:len(pairs)], refs[len(pairs):2 * len(pairs)]
-    own_q, other_q, s_ref, x_ref = refs[2 * len(pairs):]
-    seqs, width = mine[0].shape
+    seqs, width = pieces[0].shape
     half = width // 2
-    rows = s_ref.shape[0]
     total = ids.shape[1]
     own_at = pl.ds(pl.multiple_of(core * half, 128), half)
     other_at = pl.ds(pl.multiple_of((1 - core) * half, 128), half)
-
-    def place(k):
-        return pl.ds(pl.multiple_of((me ^ k) * seqs, 16), seqs)
-
-    for pair, own, other in zip(pairs, mine, theirs):
-        x_ref[place(jnp.where(core == 0, pair[0], pair[1])), :] = own[...]
-        x_ref[place(jnp.where(core == 0, pair[1], pair[0])), :] = other[...]
-    at = lax.broadcasted_iota(jnp.int32, (rows, total), 0)
-    wanted = (at // rows_each * cores + core) * rows_each + at % rows_each
-    pick = jnp.where(wanted == ids[...], 1.0, 0.0).astype(jnp.bfloat16)
-    for first, where, q_ref in ((True, own_at, own_q), (False, other_at, other_q)):
-        picked = jnp.dot(pick, x_ref[:, where], preferred_element_type=jnp.float32).astype(jnp.bfloat16)
-        part = lax.dot_general(picked, q_ref[...], NT, preferred_element_type=jnp.float32)
-        s_ref[...] = part if first else s_ref[...] + part
-
-
-def partial_scores(pairs, facts, ids, mine, theirs, own_q, other_q):
-    cores = 2
-    seqs, width = mine[0].shape
-    half = width // 2
+    for at, piece in enumerate(pieces):
+        x[at * seqs:(at + 1) * seqs, :] = piece[...]
+    part = lax.dot_general(x[:, own_at], own_q[...], NT, preferred_element_type=jnp.float32)
+    part += lax.dot_general(x[:, other_at], other_q[...], NT, preferred_element_type=jnp.float32)
+    t[...] = jnp.zeros_like(t)
+    for at, pair in enumerate(pairs):
+        rows = (me ^ jnp.where(core == 0, pair[0], pair[1])) * seqs
+        t[pl.ds(pl.multiple_of(rows, 16), seqs), :] = part[at * seqs:(at + 1) * seqs].astype(t.dtype)
+    wanted = lax.broadcasted_iota(jnp.int32, (total, total), 0)
+    pick = jnp.where(wanted == ids[...], 1.0, 0.0).astype(t.dtype)
+    s_ref[...] = jnp.dot(pick, t[...], preferred_element_type=jnp.float32).astype(s_ref.dtype)
+
+
+def partial_scores(pairs, facts, ids, pieces, own_q, other_q):
+    seqs, width = pieces[0].shape
     total = ids.shape[1]
     queries = own_q.shape[0]
-    rows = total // cores
-    rows_each = rows // (total // seqs)
-    args = [*mine, *theirs, own_q, other_q]
-    return pl.pallas_call(
-        functools.partial(score_body, pairs, rows_each, cores),
-        out_shape=[pltpu.VMEM((rows, queries), jnp.float32), pltpu.VMEM((total, 2 * half), jnp.bfloat16)],
+    args = [*pieces, own_q, other_q]
+    rows = len(pairs) * seqs
+    return pl.pallas_call(
+        functools.partial(score_body, pairs),
+        out_shape=jax.ShapeDtypeStruct((total, queries), jnp.bfloat16),
         in_specs=[SMEM] + [VMEM] * (1 + len(args)),
-        out_specs=[VMEM] * 2,
+        out_specs=VMEM,
+        scratch_shapes=[pltpu.VMEM((rows, width), jnp.bfloat16), pltpu.VMEM((total, queries), jnp.bfloat16)],
         compiler_params=pltpu.CompilerParams(vmem_limit_bytes=16 << 20),
         cost_estimate=pl.CostEstimate(
-            flops=4 * rows * queries * half, bytes_accessed=4 * half * (queries + total), transcendentals=0
+            flops=2 * rows * queries * width, bytes_accessed=2 * width * (queries + rows), transcendentals=0
         ),
         name="scores",
     )(scalars(facts), ids, *[here(arg) for arg in args])
 
 
-def fisher_body(total, facts, x_ref, f_hbm, left, out, sem):
+def fisher_body(total, facts, *refs):
+    *pieces, f_hbm, x_ref, left, out, sem = refs
+    seqs = pieces[0].shape[0]
+    for at, piece in enumerate(pieces):
+        x_ref[at * seqs:(at + 1) * seqs, :] = piece[...]
     half = x_ref.shape[1] // 2
     depth, block, _ = out.shape
     step = 512 if half % 512 == 0 else half
@@ -210,15 +208,17 @@
         copy(i).wait()
 
 
-def fisher_block(facts, x):
-    total, half = x.shape[0], x.shape[1] // 2
+def fisher_block(facts, pieces):
+    seqs, width = pieces[0].shape
+    total, half = len(pieces) * seqs, width // 2
     block, depth = (256, 4) if half % 256 == 0 and half >= 1024 else (half, 1)
     return pl.pallas_call(
         functools.partial(fisher_body, total),
         out_shape=jax.ShapeDtypeStruct((1, half, 2 * half), jnp.bfloat16),
-        in_specs=[SMEM, VMEM],
+        in_specs=[SMEM] + [VMEM] * len(pieces),
         out_specs=HBM,
         scratch_shapes=[
+            pltpu.VMEM((total, width), jnp.bfloat16),
             pltpu.VMEM((half, total), jnp.bfloat16),
             pltpu.VMEM((depth, block, 2 * half), jnp.bfloat16),
             pltpu.SemaphoreType.DMA((depth,)),
@@ -228,14 +228,17 @@
             flops=4 * total * half * half, bytes_accessed=4 * half * (half + total), transcendentals=0
         ),
         name="fisher",
-    )(scalars(facts), here(x))
+    )(scalars(facts), *[here(piece) for piece in pieces])
 
 
 def local(dp, cores, in_factor, out_factor, seq_lengths, sequence_ids, matrix_owner, queries):
-    assert cores == 2 and dp % 2 == 0 and dp & (dp - 1) == 0
+    assert cores == 2 and dp % 4 == 0 and dp & (dp - 1) == 0
     swap = [(0, 1), (1, 0)]
-    order = list(range(dp // 2, dp)) + list(range(1, dp // 2)) + [0]
-    pairs = tuple(zip(order[::2], order[1::2]))
+    distant, near = range(dp // 2, dp), range(dp // 2 - 1, -1, -1)
+    pairs = []
+    for at in range(0, dp // 2, 2):
+        pairs += [(distant[at], distant[at + 1]), (near[at], near[at + 1])]
+    pairs = tuple(pairs)
     other_in = lax.ppermute(in_factor, "mat", swap)
     in_v, out_v, own_q, facts = load(
         pairs, matrix_owner, seq_lengths, in_factor, out_factor, queries[0]
@@ -249,12 +252,16 @@
     ]
     other_q = lax.ppermute(own_q, "mat", swap)
     theirs = [lax.ppermute(piece, "mat", swap) for piece in mine]
-    part, x = partial_scores(pairs, facts, sequence_ids[None, :], mine, theirs, own_q, other_q)
+    part = partial_scores(pairs, facts, sequence_ids[None, :], mine, own_q, other_q)
     parts = lax.all_to_all(
-        part.reshape(dp, part.shape[0] // dp, -1), "dp", split_axis=0, concat_axis=0, tiled=True
+        part.reshape(dp * cores, part.shape[0] // (dp * cores), -1),
+        ("dp", "mat"),
+        split_axis=0,
+        concat_axis=0,
+        tiled=True,
     )
-    fisher = fisher_block(facts, x)
-    return (fisher, jnp.sum(parts, axis=0))
+    fisher = fisher_block(facts, mine + theirs)
+    return (fisher, jnp.sum(parts.astype(jnp.float32), axis=0))
 
 
 def solution(mesh):

time: 38.9 us -> 37.9 us (0.974)
  waiting for transfers between devices: 8.93 us -> 6.88 us
  starting transfers between devices: 15.4 us -> 16.4 us
    ppermute x4, waiting for transfers between devices: 1.33 us -> 0.01 us  [local(): theirs = [lax.ppermute(piece, 'mat', swap) for piece in mine]]
    ppermute x4, waiting for transfers between devices: 7.24 us -> 6.17 us  [local(): lax.ppermute(piece, ('dp', 'mat'), [(d * 2 + c, (d ^ pair[c]) * 2 + c) fo...]
    all_to_all x1, starting transfers between devices: 5.14 us -> 6.18 us  [local(): lax.all_to_all(part.reshape(dp * cores, part.shape[0] // (dp * cores), -1...]
  transfers between devices with their start and end apart: 11 -> 11, of which waited for: 4 -> 4; matrix products, arithmetic and copies ran while one was open for 0% -> 0% of each run, Pallas kernels for 25% -> 32%
where the time goes in v4:
time: 37.9 us; the launch traced here: 37.7 us
  starting transfers between devices  16.4 us (43%)
  Pallas kernels  13 us (34%)
  waiting for transfers between devices  6.88 us (18%)
  between operations  0.73 us (2%)
  other arithmetic  0.63 us (2%)
    ppermute x4, starting transfers between devices, local(): lax.ppermute(piece, ('dp', 'mat'), [(d * 2 + c, (d ^ pair[c]) * 2 + c) fo...  8.77 us
    pallas_call x1, Pallas kernels, fisher_block(): pl.pallas_call(functools.partial(fisher_body, total), out_shape=jax.Shape...  7.19 us
    all_to_all x1, starting transfers between devices, local(): lax.all_to_all(part.reshape(dp * cores, part.shape[0] // (dp * cores), -1...  6.18 us
    ppermute x4, waiting for transfers between devices, local(): lax.ppermute(piece, ('dp', 'mat'), [(d * 2 + c, (d ^ pair[c]) * 2 + c) fo...  6.17 us
    pallas_call x1, Pallas kernels, load(): pl.pallas_call(functools.partial(load_body, pairs), out_shape=[pltpu.VMEM...  2.59 us
    pallas_call x1, Pallas kernels, partial_scores(): pl.pallas_call(functools.partial(score_body, pairs), out_shape=jax.ShapeD...  2.21 us
    pallas_call x1, Pallas kernels, whole_slots(): pl.pallas_call(functools.partial(whole_body, n), out_shape=[pltpu.VMEM((s...  1.02 us
  transfers between devices with their start and end apart: 11, of which 4 were waited for; matrix products, arithmetic and copies ran while one was open for 0% of the time, Pallas kernels for 32%

profile of v4, /device:TPU:0, one launch (start us, length us, event | category | flops | bytes accessed | tf_op | source)
XLA Modules:
  0.0 37.7 jit_solution(9839084923081012840)
XLA Ops:
  0.6 0.5 %collective-permute-start = (bf16[16,8,32,128]{3,2,1,0:T(8,128)(2,1)}, bf16[16,8,32,128]{3,2,1,0:T(8,128)(2,1)S(1)}, u32[]{:S(2)}, u32[]{:S(2)}) collective-permute-start(bf16[16,8,32,128]{3,2,1,0:T(8,128)(2,1)} %refs_0_.1), channel_id=1, source_target_pairs={{0,1},{1,0},{2,3},{3,2},{4,5},{5,4},{6,7},{7,6},{8,9},{9,8},{10,11... | collective-permute-start | bytes 3145736 | tf_op jit(solution)/shard_map/ppermute | solution.py:242
  1.1 2.6 %load.1 = (bf16[16,8,32,128]{3,2,1,0:T(8,128)(2,1)S(1)}, bf16[16,8,64,128]{3,2,1,0:T(8,128)(2,1)S(1)}, bf16[512,2048]{1,0:T(8,128)(2,1)S(1)}, s32[22]{0:T(128)S(4)}) custom-call(s32[8]{0:T(128)} %owner_hbm.1, s32[16]{0:T(128)} %lengths_hbm.1, bf16[16,8,32,128]{3,2,1,0:T(8,128)(2,1)} %refs_0_.1, bf16[16,8,64,128]{3,2,1,0:T(8,128)(2,1)} %refs_1_.1, ...), custom_call_target="tpu_custom_call" | custom-call | tf_op jit(solution)/shard_map/load/pallas_call | solution.py:87
  3.7 0.0 collective-permute-done.other_v
  3.8 0.0 copy-start
  3.8 1.0 %whole_slots.1 = (bf16[16,4096]{1,0:T(8,128)(2,1)S(1)}, bf16[16,4096]{1,0:T(8,128)(2,1)S(1)}, bf16[16,4096]{1,0:T(8,128)(2,1)S(1)}, bf16[16,4096]{1,0:T(8,128)(2,1)S(1)}, bf16[512,2048]{1,0:T(8,128)(2,1)S(1)}) custom-call(s32[22]{0:T(128)S(4)} %get-tuple-element.11.facts, ...), custom_call_target="tpu_custom_call", output_to_operand_aliasing={{4}: (4, {})} | custom-call | flops 67108864 | bytes 2097152 | tf_op jit(solution)/shard_map/whole_slots/pallas_call | solution.py:119
  4.8 0.3 collective-permute-start.9
  5.1 3.8 %collective-permute-start.1 = (bf16[16,4096]{1,0:T(8,128)(2,1)S(1)}, bf16[16,4096]{1,0:T(8,128)(2,1)S(1)}, u32[]{:S(2)}, u32[]{:S(2)}) collective-permute-start(bf16[16,4096]{1,0:T(8,128)(2,1)S(1)} %get-tuple-element.15), channel_id=1, source_target_pairs={{0,8},{1,11},{2,10},{3,9},{4,12},{5,15},{6,14},{7,13},{8,0},{9,3},... | collective-permute-start | bytes 393224 | tf_op jit(solution)/shard_map/ppermute | solution.py:248
  9.0 2.5 %collective-permute-start.2 = (bf16[16,4096]{1,0:T(8,128)(2,1)S(1)}, bf16[16,4096]{1,0:T(8,128)(2,1)S(1)}, u32[]{:S(2)}, u32[]{:S(2)}) collective-permute-start(bf16[16,4096]{1,0:T(8,128)(2,1)S(1)} %get-tuple-element.16), channel_id=1, source_target_pairs={{0,6},{1,5},{2,4},{3,7},{4,2},{5,1},{6,0},{7,3},{8,14},{9,13},{10,... | collective-permute-start | bytes 393224 | tf_op jit(solution)/shard_map/ppermute | solution.py:248
  11.5 0.2 collective-permute-start.3
  11.7 2.2 %collective-permute-start.4 = (bf16[16,4096]{1,0:T(8,128)(2,1)S(1)}, bf16[16,4096]{1,0:T(8,128)(2,1)S(1)}, u32[]{:S(2)}, u32[]{:S(2)}) collective-permute-start(bf16[16,4096]{1,0:T(8,128)(2,1)S(1)} %get-tuple-element.18), channel_id=1, source_target_pairs={{0,2},{1,1},{2,0},{3,3},{4,6},{5,5},{6,4},{7,7},{8,10},{9,9},{10,8... | collective-permute-start | bytes 393224 | tf_op jit(solution)/shard_map/ppermute | solution.py:248
  13.9 1.8 %collective-permute-done.1.refs_0_ = bf16[16,4096]{1,0:T(8,128)(2,1)S(1)} collective-permute-done((bf16[16,4096]{1,0:T(8,128)(2,1)S(1)}, bf16[16,4096]{1,0:T(8,128)(2,1)S(1)}, u32[]{:S(2)}, u32[]{:S(2)}) %collective-permute-start.1) | collective-permute-done | bytes 131104 | tf_op jit(solution)/shard_map/ppermute | solution.py:248
  15.7 0.1 collective-permute-start.5
  15.8 0.7 %collective-permute-done.2.refs_1_ = bf16[16,4096]{1,0:T(8,128)(2,1)S(1)} collective-permute-done((bf16[16,4096]{1,0:T(8,128)(2,1)S(1)}, bf16[16,4096]{1,0:T(8,128)(2,1)S(1)}, u32[]{:S(2)}, u32[]{:S(2)}) %collective-permute-start.2) | collective-permute-done | bytes 131104 | tf_op jit(solution)/shard_map/ppermute | solution.py:248
  16.5 0.0 collective-permute-start.6
  16.5 3.7 %collective-permute-done.3.refs_2_ = bf16[16,4096]{1,0:T(8,128)(2,1)S(1)} collective-permute-done((bf16[16,4096]{1,0:T(8,128)(2,1)S(1)}, bf16[16,4096]{1,0:T(8,128)(2,1)S(1)}, u32[]{:S(2)}, u32[]{:S(2)}) %collective-permute-start.3) | collective-permute-done | bytes 131104 | tf_op jit(solution)/shard_map/ppermute | solution.py:248
  20.2 0.0 collective-permute-start.7
  20.2 0.0 collective-permute-done.4.refs_3_
  20.2 0.5 %collective-permute-start.8 = (bf16[16,4096]{1,0:T(8,128)(2,1)S(1)}, bf16[16,4096]{1,0:T(8,128)(2,1)S(1)}, u32[]{:S(2)}, u32[]{:S(2)}) collective-permute-start(bf16[16,4096]{1,0:T(8,128)(2,1)S(1)} %collective-permute-done.4.refs_3_), channel_id=1, source_target_pairs={{0,1},{1,0},{2,3},{3,2},{4,5},{5,4},{6,7},{7,6},{8,9},{9,8},{10,11... | collective-permute-start | bytes 393224 | tf_op jit(solution)/shard_map/ppermute | solution.py:254
  20.7 0.0 collective-permute-done.9.refs_5_
  20.7 0.0 copy-done
  20.7 2.2 %scores.1 = bf16[128,512]{1,0:T(8,128)(2,1)} custom-call(s32[22]{0:T(128)S(4)} %get-tuple-element.11.facts, s32[1,128]{1,0:T(1,128)S(1)} %bitcast.3, bf16[16,4096]{1,0:T(8,128)(2,1)S(1)} %collective-permute-done.1.refs_0_, bf16[16,4096]{1,0:T(8,128)(2,1)S(1)} %collective-permute-done.2.refs_1_, bf16[16,4096]{1,0:T(8,128)(2,1)S(1)} %collective-permute-done.3.refs_2_, ...), custom_call_target="tpu_custom_call" | custom-call | flops 268435456 | bytes 4718592 | tf_op jit(solution)/shard_map/scores/pallas_call | solution.py:165
  22.9 6.2 %all-to-all-start = ((bf16[16,8,512]{2,1,0:T(8,128)(2,1)}), bf16[16,8,512]{2,1,0:T(8,128)(2,1)S(1)}, u32[]{:S(2)}, u32[]{:S(2)}) async-start(bf16[16,8,512]{2,1,0:T(8,128)(2,1)} %bitcast.2), calls=%async_computation | async-start | bytes 262144 | tf_op jit(solution)/shard_map/all_to_all | solution.py:256
  29.1 0.0 collective-permute-done.5.refs_4_
  29.1 0.0 collective-permute-done.6.refs_5_
  29.1 0.0 collective-permute-done.7.refs_6_
  29.1 0.0 collective-permute-done.8.refs_7_
  29.1 7.2 %fisher.1 = bf16[1,2048,4096]{2,1,0:T(8,128)(2,1)} custom-call(s32[22]{0:T(128)S(4)} %get-tuple-element.11.facts, bf16[16,4096]{1,0:T(8,128)(2,1)S(1)} %collective-permute-done.1.refs_0_, bf16[16,4096]{1,0:T(8,128)(2,1)S(1)} %collective-permute-done.2.refs_1_, bf16[16,4096]{1,0:T(8,128)(2,1)S(1)} %collective-permute-done.3.refs_2_, ...), custom_call_target="tpu_custom_call" | custom-call | flops 2147483648 | bytes 17825792 | tf_op jit(solution)/shard_map/fisher/pallas_call | solution.py:215
  36.3 0.7 %all-to-all-done = bf16[16,8,512]{2,1,0:T(8,128)(2,1)S(1)} async-done(((bf16[16,8,512]{2,1,0:T(8,128)(2,1)}), bf16[16,8,512]{2,1,0:T(8,128)(2,1)S(1)}, u32[]{:S(2)}, u32[]{:S(2)}) %all-to-all-start) | async-done | bytes 131104 | tf_op jit(solution)/shard_map/all_to_all | solution.py:256
  37.0 0.6 %convert_reduce_fusion = f32[8,512]{1,0:T(8,128)} fusion(bf16[16,8,512]{2,1,0:T(8,128)(2,1)S(1)} %all-to-all-done), kind=kLoop, calls=%fused_computation | loop fusion | flops 126976 | bytes 147456 | tf_op jit(solution)/shard_map/reduce_sum | solution.py:264
Async XLA Ops:
  0.6 3.1 %collective-permute-start = (bf16[16,8,32,128]{3,2,1,0:T(8,128)(2,1)}, bf16[16,8,32,128]{3,2,1,0:T(8,128)(2,1)S(1)}, u32[]{:S(2)}, u32[]{:S(2)}) collective-permute-start(bf16[16,8,32,128]{3,2,1,0:T(8,128)(2,1)} %refs_0_.1), channel_id=1, source_target_pairs={{0,1},{1,0},{2,3},{3,2},{4,5},{5,4},{6,7},{7,6},{8,9},{9,8},{10,11... | collective-permute-start | bytes 3145736 | tf_op jit(solution)/shard_map/ppermute | solution.py:242
  3.8 17.0 %copy-start = (s32[128]{0:T(128)S(1)}, s32[128]{0:T(128)}, u32[]{:S(2)}) copy-start(s32[128]{0:T(128)} %param.9) | copy-start | bytes 1540
  4.8 15.9 %collective-permute-start.9 = (bf16[512,2048]{1,0:T(8,128)(2,1)S(1)}, bf16[512,2048]{1,0:T(8,128)(2,1)S(1)}, u32[]{:S(2)}, u32[]{:S(2)}) collective-permute-start(bf16[512,2048]{1,0:T(8,128)(2,1)S(1)} %get-tuple-element.19.refs_4_), channel_id=1, source_target_pairs={{0,1},{1,0},{2,3},{3,2},{4,5},{5,4},{6,7},{7,6},{8,9},{9,8},{10,11... | collective-permute-start | bytes 6291464 | tf_op jit(solution)/shard_map/ppermute | solution.py:253
  5.1 10.6 %collective-permute-start.1 = (bf16[16,4096]{1,0:T(8,128)(2,1)S(1)}, bf16[16,4096]{1,0:T(8,128)(2,1)S(1)}, u32[]{:S(2)}, u32[]{:S(2)}) collective-permute-start(bf16[16,4096]{1,0:T(8,128)(2,1)S(1)} %get-tuple-element.15), channel_id=1, source_target_pairs={{0,8},{1,11},{2,10},{3,9},{4,12},{5,15},{6,14},{7,13},{8,0},{9,3},... | collective-permute-start | bytes 393224 | tf_op jit(solution)/shard_map/ppermute | solution.py:248
  9.0 7.5 %collective-permute-start.2 = (bf16[16,4096]{1,0:T(8,128)(2,1)S(1)}, bf16[16,4096]{1,0:T(8,128)(2,1)S(1)}, u32[]{:S(2)}, u32[]{:S(2)}) collective-permute-start(bf16[16,4096]{1,0:T(8,128)(2,1)S(1)} %get-tuple-element.16), channel_id=1, source_target_pairs={{0,6},{1,5},{2,4},{3,7},{4,2},{5,1},{6,0},{7,3},{8,14},{9,13},{10,... | collective-permute-start | bytes 393224 | tf_op jit(solution)/shard_map/ppermute | solution.py:248
  11.5 8.7 %collective-permute-start.3 = (bf16[16,4096]{1,0:T(8,128)(2,1)S(1)}, bf16[16,4096]{1,0:T(8,128)(2,1)S(1)}, u32[]{:S(2)}, u32[]{:S(2)}) collective-permute-start(bf16[16,4096]{1,0:T(8,128)(2,1)S(1)} %get-tuple-element.17), channel_id=1, source_target_pairs={{0,12},{1,15},{2,14},{3,13},{4,8},{5,11},{6,10},{7,9},{8,4},{9,7},... | collective-permute-start | bytes 393224 | tf_op jit(solution)/shard_map/ppermute | solution.py:248
  11.7 8.5 %collective-permute-start.4 = (bf16[16,4096]{1,0:T(8,128)(2,1)S(1)}, bf16[16,4096]{1,0:T(8,128)(2,1)S(1)}, u32[]{:S(2)}, u32[]{:S(2)}) collective-permute-start(bf16[16,4096]{1,0:T(8,128)(2,1)S(1)} %get-tuple-element.18), channel_id=1, source_target_pairs={{0,2},{1,1},{2,0},{3,3},{4,6},{5,5},{6,4},{7,7},{8,10},{9,9},{10,8... | collective-permute-start | bytes 393224 | tf_op jit(solution)/shard_map/ppermute | solution.py:248
  15.7 13.4 %collective-permute-start.5 = (bf16[16,4096]{1,0:T(8,128)(2,1)S(1)}, bf16[16,4096]{1,0:T(8,128)(2,1)S(1)}, u32[]{:S(2)}, u32[]{:S(2)}) collective-permute-start(bf16[16,4096]{1,0:T(8,128)(2,1)S(1)} %collective-permute-done.1.refs_0_), channel_id=1, source_target_pairs={{0,1},{1,0},{2,3},{3,2},{4,5},{5,4},{6,7},{7,6},{8,9},{9,8},{10,11... | collective-permute-start | bytes 393224 | tf_op jit(solution)/shard_map/ppermute | solution.py:254
  16.5 12.6 %collective-permute-start.6 = (bf16[16,4096]{1,0:T(8,128)(2,1)S(1)}, bf16[16,4096]{1,0:T(8,128)(2,1)S(1)}, u32[]{:S(2)}, u32[]{:S(2)}) collective-permute-start(bf16[16,4096]{1,0:T(8,128)(2,1)S(1)} %collective-permute-done.2.refs_1_), channel_id=1, source_target_pairs={{0,1},{1,0},{2,3},{3,2},{4,5},{5,4},{6,7},{7,6},{8,9},{9,8},{10,11... | collective-permute-start | bytes 393224 | tf_op jit(solution)/shard_map/ppermute | solution.py:254
  20.2 8.9 %collective-permute-start.7 = (bf16[16,4096]{1,0:T(8,128)(2,1)S(1)}, bf16[16,4096]{1,0:T(8,128)(2,1)S(1)}, u32[]{:S(2)}, u32[]{:S(2)}) collective-permute-start(bf16[16,4096]{1,0:T(8,128)(2,1)S(1)} %collective-permute-done.3.refs_2_), channel_id=1, source_target_pairs={{0,1},{1,0},{2,3},{3,2},{4,5},{5,4},{6,7},{7,6},{8,9},{9,8},{10,11... | collective-permute-start | bytes 393224 | tf_op jit(solution)/shard_map/ppermute | solution.py:254
  20.2 8.9 %collective-permute-start.8 = (bf16[16,4096]{1,0:T(8,128)(2,1)S(1)}, bf16[16,4096]{1,0:T(8,128)(2,1)S(1)}, u32[]{:S(2)}, u32[]{:S(2)}) collective-permute-start(bf16[16,4096]{1,0:T(8,128)(2,1)S(1)} %collective-permute-done.4.refs_3_), channel_id=1, source_target_pairs={{0,1},{1,0},{2,3},{3,2},{4,5},{5,4},{6,7},{7,6},{8,9},{9,8},{10,11... | collective-permute-start | bytes 393224 | tf_op jit(solution)/shard_map/ppermute | solution.py:254
  22.9 14.1 %all-to-all-start = ((bf16[16,8,512]{2,1,0:T(8,128)(2,1)}), bf16[16,8,512]{2,1,0:T(8,128)(2,1)S(1)}, u32[]{:S(2)}, u32[]{:S(2)}) async-start(bf16[16,8,512]{2,1,0:T(8,128)(2,1)} %bitcast.2), calls=%async_computation | async-start | bytes 262144 | tf_op jit(solution)/shard_map/all_to_all | solution.py:256

commit v5 on v4

--- a/solution.py
+++ b/solution.py
@@ -181,28 +181,33 @@
     seqs = pieces[0].shape[0]
     for at, piece in enumerate(pieces):
         x_ref[at * seqs:(at + 1) * seqs, :] = piece[...]
-    half = x_ref.shape[1] // 2
+    width = x_ref.shape[1]
+    half = width // 2
     depth, block, _ = out.shape
-    step = 512 if half % 512 == 0 else half
-    for at in range(0, half, block):
-        where = pl.ds(pl.multiple_of(facts[0] * half + at, 128), block)
-        left[at:at + block, :] = x_ref[:, where].T
+    step = 512 if width % 512 == 0 else width
+
+    def rows_of(i):
+        return pl.ds(pl.multiple_of(i * block, block), block)
 
     def copy(i):
-        rows = pl.ds(pl.multiple_of(i * block, block), block)
-        return pltpu.make_async_copy(out.at[i % depth], f_hbm.at[0, rows], sem.at[i % depth])
-
-    @pl.loop(0, half // block)
-    def _(i):
-        @pl.when(i >= depth)
-        def _():
-            copy(i - depth).wait()
-
-        rows = left[pl.ds(pl.multiple_of(i * block, block), block), :]
-        for at in range(0, 2 * half, step):
+        return pltpu.make_async_copy(out.at[i % depth], f_hbm.at[0, rows_of(i)], sem.at[i % depth])
+
+    def make(i):
+        where = pl.ds(pl.multiple_of(facts[0] * half + i * block, 128), block)
+        left[rows_of(i), :] = x_ref[:, where].T
+        rows = left[rows_of(i), :]
+        for at in range(0, width, step):
             tile = jnp.dot(rows, x_ref[:, at:at + step], preferred_element_type=jnp.float32)
             out[i % depth, :, at:at + step] = (tile * (1.0 / total)).astype(out.dtype)
         copy(i).start()
+
+    for i in range(depth):
+        make(i)
+
+    @pl.loop(depth, half // block)
+    def _(i):
+        copy(i - depth).wait()
+        make(i)
 
     for i in range(half // block - depth, half // block):
         copy(i).wait()

time: 37.9 us -> 37.9 us (level)
  Pallas kernels: 13 us -> 12.6 us
  waiting for transfers between devices: 6.88 us -> 7.28 us
    pallas_call x1, Pallas kernels: 7.19 us -> 6.8 us  [fisher_block(): pl.pallas_call(functools.partial(fisher_body, total), out_shape=jax.Shape...]
    all_to_all x1, waiting for transfers between devices: 0.7 us -> 1.09 us  [local(): lax.all_to_all(part.reshape(dp * cores, part.shape[0] // (dp * cores), -1...]
  transfers between devices with their start and end apart: 11 -> 11, of which waited for: 4 -> 4; matrix products, arithmetic and copies ran while one was open for 0% -> 0% of each run, Pallas kernels for 32% -> 31%
where the time goes in v5:
time: 37.9 us; the launch traced here: 37.7 us
  starting transfers between devices  16.4 us (43%)
  Pallas kernels  12.6 us (33%)
  waiting for transfers between devices  7.28 us (19%)
  between operations  0.73 us (2%)
  other arithmetic  0.63 us (2%)
    ppermute x4, starting transfers between devices, local(): lax.ppermute(piece, ('dp', 'mat'), [(d * 2 + c, (d ^ pair[c]) * 2 + c) fo...  8.78 us
    pallas_call x1, Pallas kernels, fisher_block(): pl.pallas_call(functools.partial(fisher_body, total), out_shape=jax.Shape...  6.8 us
    all_to_all x1, starting transfers between devices, local(): lax.all_to_all(part.reshape(dp * cores, part.shape[0] // (dp * cores), -1...  6.18 us
    ppermute x4, waiting for transfers between devices, local(): lax.ppermute(piece, ('dp', 'mat'), [(d * 2 + c, (d ^ pair[c]) * 2 + c) fo...  6.17 us
    pallas_call x1, Pallas kernels, load(): pl.pallas_call(functools.partial(load_body, pairs), out_shape=[pltpu.VMEM...  2.59 us
    pallas_call x1, Pallas kernels, partial_scores(): pl.pallas_call(functools.partial(score_body, pairs), out_shape=jax.ShapeD...  2.21 us
    all_to_all x1, waiting for transfers between devices, local(): lax.all_to_all(part.reshape(dp * cores, part.shape[0] // (dp * cores), -1...  1.09 us
    pallas_call x1, Pallas kernels, whole_slots(): pl.pallas_call(functools.partial(whole_body, n), out_shape=[pltpu.VMEM((s...  1.03 us
  transfers between devices with their start and end apart: 11, of which 4 were waited for; matrix products, arithmetic and copies ran while one was open for 0% of the time, Pallas kernels for 31%

profile of v5, /device:TPU:0, one launch (start us, length us, event | category | flops | bytes accessed | tf_op | source)
XLA Modules:
  0.0 37.7 jit_solution(7115883819435637531)
XLA Ops:
  0.6 0.5 %collective-permute-start = (bf16[16,8,32,128]{3,2,1,0:T(8,128)(2,1)}, bf16[16,8,32,128]{3,2,1,0:T(8,128)(2,1)S(1)}, u32[]{:S(2)}, u32[]{:S(2)}) collective-permute-start(bf16[16,8,32,128]{3,2,1,0:T(8,128)(2,1)} %refs_0_.1), channel_id=1, source_target_pairs={{0,1},{1,0},{2,3},{3,2},{4,5},{5,4},{6,7},{7,6},{8,9},{9,8},{10,11... | collective-permute-start | bytes 3145736 | tf_op jit(solution)/shard_map/ppermute | solution.py:247
  1.1 2.6 %load.1 = (bf16[16,8,32,128]{3,2,1,0:T(8,128)(2,1)S(1)}, bf16[16,8,64,128]{3,2,1,0:T(8,128)(2,1)S(1)}, bf16[512,2048]{1,0:T(8,128)(2,1)S(1)}, s32[22]{0:T(128)S(4)}) custom-call(s32[8]{0:T(128)} %owner_hbm.1, s32[16]{0:T(128)} %lengths_hbm.1, bf16[16,8,32,128]{3,2,1,0:T(8,128)(2,1)} %refs_0_.1, bf16[16,8,64,128]{3,2,1,0:T(8,128)(2,1)} %refs_1_.1, ...), custom_call_target="tpu_custom_call" | custom-call | tf_op jit(solution)/shard_map/load/pallas_call | solution.py:87
  3.7 0.0 collective-permute-done.other_v
  3.8 0.0 copy-start
  3.8 1.0 %whole_slots.1 = (bf16[16,4096]{1,0:T(8,128)(2,1)S(1)}, bf16[16,4096]{1,0:T(8,128)(2,1)S(1)}, bf16[16,4096]{1,0:T(8,128)(2,1)S(1)}, bf16[16,4096]{1,0:T(8,128)(2,1)S(1)}, bf16[512,2048]{1,0:T(8,128)(2,1)S(1)}) custom-call(s32[22]{0:T(128)S(4)} %get-tuple-element.11.facts, ...), custom_call_target="tpu_custom_call", output_to_operand_aliasing={{4}: (4, {})} | custom-call | flops 67108864 | bytes 2097152 | tf_op jit(solution)/shard_map/whole_slots/pallas_call | solution.py:119
  4.8 0.3 collective-permute-start.9
  5.1 3.8 %collective-permute-start.1 = (bf16[16,4096]{1,0:T(8,128)(2,1)S(1)}, bf16[16,4096]{1,0:T(8,128)(2,1)S(1)}, u32[]{:S(2)}, u32[]{:S(2)}) collective-permute-start(bf16[16,4096]{1,0:T(8,128)(2,1)S(1)} %get-tuple-element.15), channel_id=1, source_target_pairs={{0,8},{1,11},{2,10},{3,9},{4,12},{5,15},{6,14},{7,13},{8,0},{9,3},... | collective-permute-start | bytes 393224 | tf_op jit(solution)/shard_map/ppermute | solution.py:253
  9.0 2.5 %collective-permute-start.2 = (bf16[16,4096]{1,0:T(8,128)(2,1)S(1)}, bf16[16,4096]{1,0:T(8,128)(2,1)S(1)}, u32[]{:S(2)}, u32[]{:S(2)}) collective-permute-start(bf16[16,4096]{1,0:T(8,128)(2,1)S(1)} %get-tuple-element.16), channel_id=1, source_target_pairs={{0,6},{1,5},{2,4},{3,7},{4,2},{5,1},{6,0},{7,3},{8,14},{9,13},{10,... | collective-permute-start | bytes 393224 | tf_op jit(solution)/shard_map/ppermute | solution.py:253
  11.5 0.2 collective-permute-start.3
  11.7 2.2 %collective-permute-start.4 = (bf16[16,4096]{1,0:T(8,128)(2,1)S(1)}, bf16[16,4096]{1,0:T(8,128)(2,1)S(1)}, u32[]{:S(2)}, u32[]{:S(2)}) collective-permute-start(bf16[16,4096]{1,0:T(8,128)(2,1)S(1)} %get-tuple-element.18), channel_id=1, source_target_pairs={{0,2},{1,1},{2,0},{3,3},{4,6},{5,5},{6,4},{7,7},{8,10},{9,9},{10,8... | collective-permute-start | bytes 393224 | tf_op jit(solution)/shard_map/ppermute | solution.py:253
  13.9 1.8 %collective-permute-done.1.refs_0_ = bf16[16,4096]{1,0:T(8,128)(2,1)S(1)} collective-permute-done((bf16[16,4096]{1,0:T(8,128)(2,1)S(1)}, bf16[16,4096]{1,0:T(8,128)(2,1)S(1)}, u32[]{:S(2)}, u32[]{:S(2)}) %collective-permute-start.1) | collective-permute-done | bytes 131104 | tf_op jit(solution)/shard_map/ppermute | solution.py:253
  15.7 0.1 collective-permute-start.5
  15.8 0.7 %collective-permute-done.2.refs_1_ = bf16[16,4096]{1,0:T(8,128)(2,1)S(1)} collective-permute-done((bf16[16,4096]{1,0:T(8,128)(2,1)S(1)}, bf16[16,4096]{1,0:T(8,128)(2,1)S(1)}, u32[]{:S(2)}, u32[]{:S(2)}) %collective-permute-start.2) | collective-permute-done | bytes 131104 | tf_op jit(solution)/shard_map/ppermute | solution.py:253
  16.5 0.0 collective-permute-start.6
  16.5 3.7 %collective-permute-done.3.refs_2_ = bf16[16,4096]{1,0:T(8,128)(2,1)S(1)} collective-permute-done((bf16[16,4096]{1,0:T(8,128)(2,1)S(1)}, bf16[16,4096]{1,0:T(8,128)(2,1)S(1)}, u32[]{:S(2)}, u32[]{:S(2)}) %collective-permute-start.3) | collective-permute-done | bytes 131104 | tf_op jit(solution)/shard_map/ppermute | solution.py:253
  20.2 0.0 collective-permute-start.7
  20.2 0.0 collective-permute-done.4.refs_3_
  20.2 0.5 %collective-permute-start.8 = (bf16[16,4096]{1,0:T(8,128)(2,1)S(1)}, bf16[16,4096]{1,0:T(8,128)(2,1)S(1)}, u32[]{:S(2)}, u32[]{:S(2)}) collective-permute-start(bf16[16,4096]{1,0:T(8,128)(2,1)S(1)} %collective-permute-done.4.refs_3_), channel_id=1, source_target_pairs={{0,1},{1,0},{2,3},{3,2},{4,5},{5,4},{6,7},{7,6},{8,9},{9,8},{10,11... | collective-permute-start | bytes 393224 | tf_op jit(solution)/shard_map/ppermute | solution.py:259
  20.7 0.0 collective-permute-done.9.refs_5_
  20.7 0.0 copy-done
  20.7 2.2 %scores.1 = bf16[128,512]{1,0:T(8,128)(2,1)} custom-call(s32[22]{0:T(128)S(4)} %get-tuple-element.11.facts, s32[1,128]{1,0:T(1,128)S(1)} %bitcast.3, bf16[16,4096]{1,0:T(8,128)(2,1)S(1)} %collective-permute-done.1.refs_0_, bf16[16,4096]{1,0:T(8,128)(2,1)S(1)} %collective-permute-done.2.refs_1_, bf16[16,4096]{1,0:T(8,128)(2,1)S(1)} %collective-permute-done.3.refs_2_, ...), custom_call_target="tpu_custom_call" | custom-call | flops 268435456 | bytes 4718592 | tf_op jit(solution)/shard_map/scores/pallas_call | solution.py:165
  22.9 6.2 %all-to-all-start = ((bf16[16,8,512]{2,1,0:T(8,128)(2,1)}), bf16[16,8,512]{2,1,0:T(8,128)(2,1)S(1)}, u32[]{:S(2)}, u32[]{:S(2)}) async-start(bf16[16,8,512]{2,1,0:T(8,128)(2,1)} %bitcast.2), calls=%async_computation | async-start | bytes 262144 | tf_op jit(solution)/shard_map/all_to_all | solution.py:261
  29.1 0.0 collective-permute-done.5.refs_4_
  29.1 0.0 collective-permute-done.6.refs_5_
  29.1 0.0 collective-permute-done.7.refs_6_
  29.1 0.0 collective-permute-done.8.refs_7_
  29.1 6.8 %fisher.1 = bf16[1,2048,4096]{2,1,0:T(8,128)(2,1)} custom-call(s32[22]{0:T(128)S(4)} %get-tuple-element.11.facts, bf16[16,4096]{1,0:T(8,128)(2,1)S(1)} %collective-permute-done.1.refs_0_, bf16[16,4096]{1,0:T(8,128)(2,1)S(1)} %collective-permute-done.2.refs_1_, bf16[16,4096]{1,0:T(8,128)(2,1)S(1)} %collective-permute-done.3.refs_2_, ...), custom_call_target="tpu_custom_call" | custom-call | flops 2147483648 | bytes 17825792 | tf_op jit(solution)/shard_map/fisher/pallas_call | solution.py:220
  35.9 1.1 %all-to-all-done = bf16[16,8,512]{2,1,0:T(8,128)(2,1)S(1)} async-done(((bf16[16,8,512]{2,1,0:T(8,128)(2,1)}), bf16[16,8,512]{2,1,0:T(8,128)(2,1)S(1)}, u32[]{:S(2)}, u32[]{:S(2)}) %all-to-all-start) | async-done | bytes 131104 | tf_op jit(solution)/shard_map/all_to_all | solution.py:261
  37.0 0.6 %convert_reduce_fusion = f32[8,512]{1,0:T(8,128)} fusion(bf16[16,8,512]{2,1,0:T(8,128)(2,1)S(1)} %all-to-all-done), kind=kLoop, calls=%fused_computation | loop fusion | flops 126976 | bytes 147456 | tf_op jit(solution)/shard_map/reduce_sum | solution.py:269
Async XLA Ops:
  0.6 3.1 %collective-permute-start = (bf16[16,8,32,128]{3,2,1,0:T(8,128)(2,1)}, bf16[16,8,32,128]{3,2,1,0:T(8,128)(2,1)S(1)}, u32[]{:S(2)}, u32[]{:S(2)}) collective-permute-start(bf16[16,8,32,128]{3,2,1,0:T(8,128)(2,1)} %refs_0_.1), channel_id=1, source_target_pairs={{0,1},{1,0},{2,3},{3,2},{4,5},{5,4},{6,7},{7,6},{8,9},{9,8},{10,11... | collective-permute-start | bytes 3145736 | tf_op jit(solution)/shard_map/ppermute | solution.py:247
  3.8 17.0 %copy-start = (s32[128]{0:T(128)S(1)}, s32[128]{0:T(128)}, u32[]{:S(2)}) copy-start(s32[128]{0:T(128)} %param.9) | copy-start | bytes 1540
  4.8 15.9 %collective-permute-start.9 = (bf16[512,2048]{1,0:T(8,128)(2,1)S(1)}, bf16[512,2048]{1,0:T(8,128)(2,1)S(1)}, u32[]{:S(2)}, u32[]{:S(2)}) collective-permute-start(bf16[512,2048]{1,0:T(8,128)(2,1)S(1)} %get-tuple-element.19.refs_4_), channel_id=1, source_target_pairs={{0,1},{1,0},{2,3},{3,2},{4,5},{5,4},{6,7},{7,6},{8,9},{9,8},{10,11... | collective-permute-start | bytes 6291464 | tf_op jit(solution)/shard_map/ppermute | solution.py:258
  5.1 10.6 %collective-permute-start.1 = (bf16[16,4096]{1,0:T(8,128)(2,1)S(1)}, bf16[16,4096]{1,0:T(8,128)(2,1)S(1)}, u32[]{:S(2)}, u32[]{:S(2)}) collective-permute-start(bf16[16,4096]{1,0:T(8,128)(2,1)S(1)} %get-tuple-element.15), channel_id=1, source_target_pairs={{0,8},{1,11},{2,10},{3,9},{4,12},{5,15},{6,14},{7,13},{8,0},{9,3},... | collective-permute-start | bytes 393224 | tf_op jit(solution)/shard_map/ppermute | solution.py:253
  9.0 7.5 %collective-permute-start.2 = (bf16[16,4096]{1,0:T(8,128)(2,1)S(1)}, bf16[16,4096]{1,0:T(8,128)(2,1)S(1)}, u32[]{:S(2)}, u32[]{:S(2)}) collective-permute-start(bf16[16,4096]{1,0:T(8,128)(2,1)S(1)} %get-tuple-element.16), channel_id=1, source_target_pairs={{0,6},{1,5},{2,4},{3,7},{4,2},{5,1},{6,0},{7,3},{8,14},{9,13},{10,... | collective-permute-start | bytes 393224 | tf_op jit(solution)/shard_map/ppermute | solution.py:253
  11.5 8.7 %collective-permute-start.3 = (bf16[16,4096]{1,0:T(8,128)(2,1)S(1)}, bf16[16,4096]{1,0:T(8,128)(2,1)S(1)}, u32[]{:S(2)}, u32[]{:S(2)}) collective-permute-start(bf16[16,4096]{1,0:T(8,128)(2,1)S(1)} %get-tuple-element.17), channel_id=1, source_target_pairs={{0,12},{1,15},{2,14},{3,13},{4,8},{5,11},{6,10},{7,9},{8,4},{9,7},... | collective-permute-start | bytes 393224 | tf_op jit(solution)/shard_map/ppermute | solution.py:253
  11.7 8.5 %collective-permute-start.4 = (bf16[16,4096]{1,0:T(8,128)(2,1)S(1)}, bf16[16,4096]{1,0:T(8,128)(2,1)S(1)}, u32[]{:S(2)}, u32[]{:S(2)}) collective-permute-start(bf16[16,4096]{1,0:T(8,128)(2,1)S(1)} %get-tuple-element.18), channel_id=1, source_target_pairs={{0,2},{1,1},{2,0},{3,3},{4,6},{5,5},{6,4},{7,7},{8,10},{9,9},{10,8... | collective-permute-start | bytes 393224 | tf_op jit(solution)/shard_map/ppermute | solution.py:253
  15.7 13.4 %collective-permute-start.5 = (bf16[16,4096]{1,0:T(8,128)(2,1)S(1)}, bf16[16,4096]{1,0:T(8,128)(2,1)S(1)}, u32[]{:S(2)}, u32[]{:S(2)}) collective-permute-start(bf16[16,4096]{1,0:T(8,128)(2,1)S(1)} %collective-permute-done.1.refs_0_), channel_id=1, source_target_pairs={{0,1},{1,0},{2,3},{3,2},{4,5},{5,4},{6,7},{7,6},{8,9},{9,8},{10,11... | collective-permute-start | bytes 393224 | tf_op jit(solution)/shard_map/ppermute | solution.py:259
  16.5 12.6 %collective-permute-start.6 = (bf16[16,4096]{1,0:T(8,128)(2,1)S(1)}, bf16[16,4096]{1,0:T(8,128)(2,1)S(1)}, u32[]{:S(2)}, u32[]{:S(2)}) collective-permute-start(bf16[16,4096]{1,0:T(8,128)(2,1)S(1)} %collective-permute-done.2.refs_1_), channel_id=1, source_target_pairs={{0,1},{1,0},{2,3},{3,2},{4,5},{5,4},{6,7},{7,6},{8,9},{9,8},{10,11... | collective-permute-start | bytes 393224 | tf_op jit(solution)/shard_map/ppermute | solution.py:259
  20.2 8.9 %collective-permute-start.7 = (bf16[16,4096]{1,0:T(8,128)(2,1)S(1)}, bf16[16,4096]{1,0:T(8,128)(2,1)S(1)}, u32[]{:S(2)}, u32[]{:S(2)}) collective-permute-start(bf16[16,4096]{1,0:T(8,128)(2,1)S(1)} %collective-permute-done.3.refs_2_), channel_id=1, source_target_pairs={{0,1},{1,0},{2,3},{3,2},{4,5},{5,4},{6,7},{7,6},{8,9},{9,8},{10,11... | collective-permute-start | bytes 393224 | tf_op jit(solution)/shard_map/ppermute | solution.py:259
  20.2 8.9 %collective-permute-start.8 = (bf16[16,4096]{1,0:T(8,128)(2,1)S(1)}, bf16[16,4096]{1,0:T(8,128)(2,1)S(1)}, u32[]{:S(2)}, u32[]{:S(2)}) collective-permute-start(bf16[16,4096]{1,0:T(8,128)(2,1)S(1)} %collective-permute-done.4.refs_3_), channel_id=1, source_target_pairs={{0,1},{1,0},{2,3},{3,2},{4,5},{5,4},{6,7},{7,6},{8,9},{9,8},{10,11... | collective-permute-start | bytes 393224 | tf_op jit(solution)/shard_map/ppermute | solution.py:259
  22.9 14.1 %all-to-all-start = ((bf16[16,8,512]{2,1,0:T(8,128)(2,1)}), bf16[16,8,512]{2,1,0:T(8,128)(2,1)S(1)}, u32[]{:S(2)}, u32[]{:S(2)}) async-start(bf16[16,8,512]{2,1,0:T(8,128)(2,1)} %bitcast.2), calls=%async_computation | async-start | bytes 262144 | tf_op jit(solution)/shard_map/all_to_all | solution.py:261

commit v6 on v5

--- a/solution.py
+++ b/solution.py
@@ -8,7 +8,6 @@
 from jax.sharding import PartitionSpec as P
 
 NT = (((1,), (1,)), ((), ()))
-TN = (((0,), (0,)), ((), ()))
 VMEM = pl.BlockSpec(memory_space=pltpu.VMEM)
 SMEM = pl.BlockSpec(memory_space=pltpu.SMEM)
 HBM = pl.BlockSpec(memory_space=pl.ANY)
@@ -36,7 +35,7 @@
 def slot_rows(in_v, other_v, out_v, matrix, length_of, tiles, store):
     seqs, _, width, length = out_v.shape
     rows = 2 * in_v.shape[2]
-    stride = tiles.shape[0] // seqs
+    stride = tiles.shape[0] // (seqs + 1)
     per = length // width
     scale = length ** (-0.5)
     lane = lax.broadcasted_iota(jnp.int32, (1, length), 1)
@@ -123,7 +122,7 @@
         in_specs=[SMEM] + [VMEM] * 4,
         out_specs=[VMEM] * (n + 1),
         input_output_aliases={4: n},
-        scratch_shapes=[pltpu.VMEM((2, seqs * (2 * rows + 8), length), jnp.float32)],
+        scratch_shapes=[pltpu.VMEM((2, (seqs + 1) * (2 * rows + 8), length), jnp.float32)],
         compiler_params=pltpu.CompilerParams(vmem_limit_bytes=12 << 20),
         cost_estimate=pl.CostEstimate(
             flops=4 * n * seqs * rows * width * length,

time: 37.9 us -> 37.9 us (level)
  no operation moved by 1% of the time
where the time goes in v6:
time: 37.9 us; the launch traced here: 37.7 us
  starting transfers between devices  16.4 us (43%)
  Pallas kernels  12.6 us (33%)
  waiting for transfers between devices  7.28 us (19%)
  between operations  0.73 us (2%)
  other arithmetic  0.63 us (2%)
    ppermute x4, starting transfers between devices, local(): lax.ppermute(piece, ('dp', 'mat'), [(d * 2 + c, (d ^ pair[c]) * 2 + c) fo...  8.79 us
    pallas_call x1, Pallas kernels, fisher_block(): pl.pallas_call(functools.partial(fisher_body, total), out_shape=jax.Shape...  6.8 us
    all_to_all x1, starting transfers between devices, local(): lax.all_to_all(part.reshape(dp * cores, part.shape[0] // (dp * cores), -1...  6.19 us
    ppermute x4, waiting for transfers between devices, local(): lax.ppermute(piece, ('dp', 'mat'), [(d * 2 + c, (d ^ pair[c]) * 2 + c) fo...  6.18 us
    pallas_call x1, Pallas kernels, load(): pl.pallas_call(functools.partial(load_body, pairs), out_shape=[pltpu.VMEM...  2.59 us
    pallas_call x1, Pallas kernels, partial_scores(): pl.pallas_call(functools.partial(score_body, pairs), out_shape=jax.ShapeD...  2.21 us
    all_to_all x1, waiting for transfers between devices, local(): lax.all_to_all(part.reshape(dp * cores, part.shape[0] // (dp * cores), -1...  1.09 us
    pallas_call x1, Pallas kernels, whole_slots(): pl.pallas_call(functools.partial(whole_body, n), out_shape=[pltpu.VMEM((s...  1.01 us
  transfers between devices with their start and end apart: 11, of which 4 were waited for; matrix products, arithmetic and copies ran while one was open for 0% of the time, Pallas kernels for 31%

profile of v6, /device:TPU:0, one launch (start us, length us, event | category | flops | bytes accessed | tf_op | source)
XLA Modules:
  0.0 37.7 jit_solution(13312267754342728925)
XLA Ops:
  0.6 0.5 %collective-permute-start = (bf16[16,8,32,128]{3,2,1,0:T(8,128)(2,1)}, bf16[16,8,32,128]{3,2,1,0:T(8,128)(2,1)S(1)}, u32[]{:S(2)}, u32[]{:S(2)}) collective-permute-start(bf16[16,8,32,128]{3,2,1,0:T(8,128)(2,1)} %refs_0_.1), channel_id=1, source_target_pairs={{0,1},{1,0},{2,3},{3,2},{4,5},{5,4},{6,7},{7,6},{8,9},{9,8},{10,11... | collective-permute-start | bytes 3145736 | tf_op jit(solution)/shard_map/ppermute | solution.py:246
  1.1 2.6 %load.1 = (bf16[16,8,32,128]{3,2,1,0:T(8,128)(2,1)S(1)}, bf16[16,8,64,128]{3,2,1,0:T(8,128)(2,1)S(1)}, bf16[512,2048]{1,0:T(8,128)(2,1)S(1)}, s32[22]{0:T(128)S(4)}) custom-call(s32[8]{0:T(128)} %owner_hbm.1, s32[16]{0:T(128)} %lengths_hbm.1, bf16[16,8,32,128]{3,2,1,0:T(8,128)(2,1)} %refs_0_.1, bf16[16,8,64,128]{3,2,1,0:T(8,128)(2,1)} %refs_1_.1, ...), custom_call_target="tpu_custom_call" | custom-call | tf_op jit(solution)/shard_map/load/pallas_call | solution.py:86
  3.7 0.0 collective-permute-done.other_v
  3.8 0.0 copy-start
  3.8 1.0 %whole_slots.1 = (bf16[16,4096]{1,0:T(8,128)(2,1)S(1)}, bf16[16,4096]{1,0:T(8,128)(2,1)S(1)}, bf16[16,4096]{1,0:T(8,128)(2,1)S(1)}, bf16[16,4096]{1,0:T(8,128)(2,1)S(1)}, bf16[512,2048]{1,0:T(8,128)(2,1)S(1)}) custom-call(s32[22]{0:T(128)S(4)} %get-tuple-element.11.facts, ...), custom_call_target="tpu_custom_call", output_to_operand_aliasing={{4}: (4, {})} | custom-call | flops 67108864 | bytes 2097152 | tf_op jit(solution)/shard_map/whole_slots/pallas_call | solution.py:118
  4.8 0.3 collective-permute-start.9
  5.1 3.9 %collective-permute-start.1 = (bf16[16,4096]{1,0:T(8,128)(2,1)S(1)}, bf16[16,4096]{1,0:T(8,128)(2,1)S(1)}, u32[]{:S(2)}, u32[]{:S(2)}) collective-permute-start(bf16[16,4096]{1,0:T(8,128)(2,1)S(1)} %get-tuple-element.15), channel_id=1, source_target_pairs={{0,8},{1,11},{2,10},{3,9},{4,12},{5,15},{6,14},{7,13},{8,0},{9,3},... | collective-permute-start | bytes 393224 | tf_op jit(solution)/shard_map/ppermute | solution.py:252
  9.0 2.5 %collective-permute-start.2 = (bf16[16,4096]{1,0:T(8,128)(2,1)S(1)}, bf16[16,4096]{1,0:T(8,128)(2,1)S(1)}, u32[]{:S(2)}, u32[]{:S(2)}) collective-permute-start(bf16[16,4096]{1,0:T(8,128)(2,1)S(1)} %get-tuple-element.16), channel_id=1, source_target_pairs={{0,6},{1,5},{2,4},{3,7},{4,2},{5,1},{6,0},{7,3},{8,14},{9,13},{10,... | collective-permute-start | bytes 393224 | tf_op jit(solution)/shard_map/ppermute | solution.py:252
  11.5 0.2 collective-permute-start.3
  11.7 2.2 %collective-permute-start.4 = (bf16[16,4096]{1,0:T(8,128)(2,1)S(1)}, bf16[16,4096]{1,0:T(8,128)(2,1)S(1)}, u32[]{:S(2)}, u32[]{:S(2)}) collective-permute-start(bf16[16,4096]{1,0:T(8,128)(2,1)S(1)} %get-tuple-element.18), channel_id=1, source_target_pairs={{0,2},{1,1},{2,0},{3,3},{4,6},{5,5},{6,4},{7,7},{8,10},{9,9},{10,8... | collective-permute-start | bytes 393224 | tf_op jit(solution)/shard_map/ppermute | solution.py:252
  13.9 1.8 %collective-permute-done.1.refs_0_ = bf16[16,4096]{1,0:T(8,128)(2,1)S(1)} collective-permute-done((bf16[16,4096]{1,0:T(8,128)(2,1)S(1)}, bf16[16,4096]{1,0:T(8,128)(2,1)S(1)}, u32[]{:S(2)}, u32[]{:S(2)}) %collective-permute-start.1) | collective-permute-done | bytes 131104 | tf_op jit(solution)/shard_map/ppermute | solution.py:252
  15.7 0.1 collective-permute-start.5
  15.8 0.6 %collective-permute-done.2.refs_1_ = bf16[16,4096]{1,0:T(8,128)(2,1)S(1)} collective-permute-done((bf16[16,4096]{1,0:T(8,128)(2,1)S(1)}, bf16[16,4096]{1,0:T(8,128)(2,1)S(1)}, u32[]{:S(2)}, u32[]{:S(2)}) %collective-permute-start.2) | collective-permute-done | bytes 131104 | tf_op jit(solution)/shard_map/ppermute | solution.py:252
  16.4 0.0 collective-permute-start.6
  16.4 3.7 %collective-permute-done.3.refs_2_ = bf16[16,4096]{1,0:T(8,128)(2,1)S(1)} collective-permute-done((bf16[16,4096]{1,0:T(8,128)(2,1)S(1)}, bf16[16,4096]{1,0:T(8,128)(2,1)S(1)}, u32[]{:S(2)}, u32[]{:S(2)}) %collective-permute-start.3) | collective-permute-done | bytes 131104 | tf_op jit(solution)/shard_map/ppermute | solution.py:252
  20.2 0.0 collective-permute-start.7
  20.2 0.0 collective-permute-done.4.refs_3_
  20.2 0.5 %collective-permute-start.8 = (bf16[16,4096]{1,0:T(8,128)(2,1)S(1)}, bf16[16,4096]{1,0:T(8,128)(2,1)S(1)}, u32[]{:S(2)}, u32[]{:S(2)}) collective-permute-start(bf16[16,4096]{1,0:T(8,128)(2,1)S(1)} %collective-permute-done.4.refs_3_), channel_id=1, source_target_pairs={{0,1},{1,0},{2,3},{3,2},{4,5},{5,4},{6,7},{7,6},{8,9},{9,8},{10,11... | collective-permute-start | bytes 393224 | tf_op jit(solution)/shard_map/ppermute | solution.py:258
  20.7 0.0 collective-permute-done.9.refs_5_
  20.7 0.0 copy-done
  20.7 2.2 %scores.1 = bf16[128,512]{1,0:T(8,128)(2,1)} custom-call(s32[22]{0:T(128)S(4)} %get-tuple-element.11.facts, s32[1,128]{1,0:T(1,128)S(1)} %bitcast.3, bf16[16,4096]{1,0:T(8,128)(2,1)S(1)} %collective-permute-done.1.refs_0_, bf16[16,4096]{1,0:T(8,128)(2,1)S(1)} %collective-permute-done.2.refs_1_, bf16[16,4096]{1,0:T(8,128)(2,1)S(1)} %collective-permute-done.3.refs_2_, ...), custom_call_target="tpu_custom_call" | custom-call | flops 268435456 | bytes 4718592 | tf_op jit(solution)/shard_map/scores/pallas_call | solution.py:164
  22.9 6.2 %all-to-all-start = ((bf16[16,8,512]{2,1,0:T(8,128)(2,1)}), bf16[16,8,512]{2,1,0:T(8,128)(2,1)S(1)}, u32[]{:S(2)}, u32[]{:S(2)}) async-start(bf16[16,8,512]{2,1,0:T(8,128)(2,1)} %bitcast.2), calls=%async_computation | async-start | bytes 262144 | tf_op jit(solution)/shard_map/all_to_all | solution.py:260
  29.1 0.0 collective-permute-done.5.refs_4_
  29.1 0.0 collective-permute-done.6.refs_5_
  29.1 0.0 collective-permute-done.7.refs_6_
  29.1 0.0 collective-permute-done.8.refs_7_
  29.1 6.8 %fisher.1 = bf16[1,2048,4096]{2,1,0:T(8,128)(2,1)} custom-call(s32[22]{0:T(128)S(4)} %get-tuple-element.11.facts, bf16[16,4096]{1,0:T(8,128)(2,1)S(1)} %collective-permute-done.1.refs_0_, bf16[16,4096]{1,0:T(8,128)(2,1)S(1)} %collective-permute-done.2.refs_1_, bf16[16,4096]{1,0:T(8,128)(2,1)S(1)} %collective-permute-done.3.refs_2_, ...), custom_call_target="tpu_custom_call" | custom-call | flops 2147483648 | bytes 17825792 | tf_op jit(solution)/shard_map/fisher/pallas_call | solution.py:219
  35.9 1.1 %all-to-all-done = bf16[16,8,512]{2,1,0:T(8,128)(2,1)S(1)} async-done(((bf16[16,8,512]{2,1,0:T(8,128)(2,1)}), bf16[16,8,512]{2,1,0:T(8,128)(2,1)S(1)}, u32[]{:S(2)}, u32[]{:S(2)}) %all-to-all-start) | async-done | bytes 131104 | tf_op jit(solution)/shard_map/all_to_all | solution.py:260
  37.0 0.6 %convert_reduce_fusion = f32[8,512]{1,0:T(8,128)} fusion(bf16[16,8,512]{2,1,0:T(8,128)(2,1)S(1)} %all-to-all-done), kind=kLoop, calls=%fused_computation | loop fusion | flops 126976 | bytes 147456 | tf_op jit(solution)/shard_map/reduce_sum | solution.py:268
Async XLA Ops:
  0.6 3.1 %collective-permute-start = (bf16[16,8,32,128]{3,2,1,0:T(8,128)(2,1)}, bf16[16,8,32,128]{3,2,1,0:T(8,128)(2,1)S(1)}, u32[]{:S(2)}, u32[]{:S(2)}) collective-permute-start(bf16[16,8,32,128]{3,2,1,0:T(8,128)(2,1)} %refs_0_.1), channel_id=1, source_target_pairs={{0,1},{1,0},{2,3},{3,2},{4,5},{5,4},{6,7},{7,6},{8,9},{9,8},{10,11... | collective-permute-start | bytes 3145736 | tf_op jit(solution)/shard_map/ppermute | solution.py:246
  3.8 16.9 %copy-start = (s32[128]{0:T(128)S(1)}, s32[128]{0:T(128)}, u32[]{:S(2)}) copy-start(s32[128]{0:T(128)} %param.9) | copy-start | bytes 1540
  4.8 15.9 %collective-permute-start.9 = (bf16[512,2048]{1,0:T(8,128)(2,1)S(1)}, bf16[512,2048]{1,0:T(8,128)(2,1)S(1)}, u32[]{:S(2)}, u32[]{:S(2)}) collective-permute-start(bf16[512,2048]{1,0:T(8,128)(2,1)S(1)} %get-tuple-element.19.refs_4_), channel_id=1, source_target_pairs={{0,1},{1,0},{2,3},{3,2},{4,5},{5,4},{6,7},{7,6},{8,9},{9,8},{10,11... | collective-permute-start | bytes 6291464 | tf_op jit(solution)/shard_map/ppermute | solution.py:257
  5.1 10.6 %collective-permute-start.1 = (bf16[16,4096]{1,0:T(8,128)(2,1)S(1)}, bf16[16,4096]{1,0:T(8,128)(2,1)S(1)}, u32[]{:S(2)}, u32[]{:S(2)}) collective-permute-start(bf16[16,4096]{1,0:T(8,128)(2,1)S(1)} %get-tuple-element.15), channel_id=1, source_target_pairs={{0,8},{1,11},{2,10},{3,9},{4,12},{5,15},{6,14},{7,13},{8,0},{9,3},... | collective-permute-start | bytes 393224 | tf_op jit(solution)/shard_map/ppermute | solution.py:252
  9.0 7.5 %collective-permute-start.2 = (bf16[16,4096]{1,0:T(8,128)(2,1)S(1)}, bf16[16,4096]{1,0:T(8,128)(2,1)S(1)}, u32[]{:S(2)}, u32[]{:S(2)}) collective-permute-start(bf16[16,4096]{1,0:T(8,128)(2,1)S(1)} %get-tuple-element.16), channel_id=1, source_target_pairs={{0,6},{1,5},{2,4},{3,7},{4,2},{5,1},{6,0},{7,3},{8,14},{9,13},{10,... | collective-permute-start | bytes 393224 | tf_op jit(solution)/shard_map/ppermute | solution.py:252
  11.5 8.7 %collective-permute-start.3 = (bf16[16,4096]{1,0:T(8,128)(2,1)S(1)}, bf16[16,4096]{1,0:T(8,128)(2,1)S(1)}, u32[]{:S(2)}, u32[]{:S(2)}) collective-permute-start(bf16[16,4096]{1,0:T(8,128)(2,1)S(1)} %get-tuple-element.17), channel_id=1, source_target_pairs={{0,12},{1,15},{2,14},{3,13},{4,8},{5,11},{6,10},{7,9},{8,4},{9,7},... | collective-permute-start | bytes 393224 | tf_op jit(solution)/shard_map/ppermute | solution.py:252
  11.7 8.5 %collective-permute-start.4 = (bf16[16,4096]{1,0:T(8,128)(2,1)S(1)}, bf16[16,4096]{1,0:T(8,128)(2,1)S(1)}, u32[]{:S(2)}, u32[]{:S(2)}) collective-permute-start(bf16[16,4096]{1,0:T(8,128)(2,1)S(1)} %get-tuple-element.18), channel_id=1, source_target_pairs={{0,2},{1,1},{2,0},{3,3},{4,6},{5,5},{6,4},{7,7},{8,10},{9,9},{10,8... | collective-permute-start | bytes 393224 | tf_op jit(solution)/shard_map/ppermute | solution.py:252
  15.7 13.4 %collective-permute-start.5 = (bf16[16,4096]{1,0:T(8,128)(2,1)S(1)}, bf16[16,4096]{1,0:T(8,128)(2,1)S(1)}, u32[]{:S(2)}, u32[]{:S(2)}) collective-permute-start(bf16[16,4096]{1,0:T(8,128)(2,1)S(1)} %collective-permute-done.1.refs_0_), channel_id=1, source_target_pairs={{0,1},{1,0},{2,3},{3,2},{4,5},{5,4},{6,7},{7,6},{8,9},{9,8},{10,11... | collective-permute-start | bytes 393224 | tf_op jit(solution)/shard_map/ppermute | solution.py:258
  16.4 12.7 %collective-permute-start.6 = (bf16[16,4096]{1,0:T(8,128)(2,1)S(1)}, bf16[16,4096]{1,0:T(8,128)(2,1)S(1)}, u32[]{:S(2)}, u32[]{:S(2)}) collective-permute-start(bf16[16,4096]{1,0:T(8,128)(2,1)S(1)} %collective-permute-done.2.refs_1_), channel_id=1, source_target_pairs={{0,1},{1,0},{2,3},{3,2},{4,5},{5,4},{6,7},{7,6},{8,9},{9,8},{10,11... | collective-permute-start | bytes 393224 | tf_op jit(solution)/shard_map/ppermute | solution.py:258
  20.2 9.0 %collective-permute-start.7 = (bf16[16,4096]{1,0:T(8,128)(2,1)S(1)}, bf16[16,4096]{1,0:T(8,128)(2,1)S(1)}, u32[]{:S(2)}, u32[]{:S(2)}) collective-permute-start(bf16[16,4096]{1,0:T(8,128)(2,1)S(1)} %collective-permute-done.3.refs_2_), channel_id=1, source_target_pairs={{0,1},{1,0},{2,3},{3,2},{4,5},{5,4},{6,7},{7,6},{8,9},{9,8},{10,11... | collective-permute-start | bytes 393224 | tf_op jit(solution)/shard_map/ppermute | solution.py:258
  20.2 9.0 %collective-permute-start.8 = (bf16[16,4096]{1,0:T(8,128)(2,1)S(1)}, bf16[16,4096]{1,0:T(8,128)(2,1)S(1)}, u32[]{:S(2)}, u32[]{:S(2)}) collective-permute-start(bf16[16,4096]{1,0:T(8,128)(2,1)S(1)} %collective-permute-done.4.refs_3_), channel_id=1, source_target_pairs={{0,1},{1,0},{2,3},{3,2},{4,5},{5,4},{6,7},{7,6},{8,9},{9,8},{10,11... | collective-permute-start | bytes 393224 | tf_op jit(solution)/shard_map/ppermute | solution.py:258
  22.9 14.1 %all-to-all-start = ((bf16[16,8,512]{2,1,0:T(8,128)(2,1)}), bf16[16,8,512]{2,1,0:T(8,128)(2,1)S(1)}, u32[]{:S(2)}, u32[]{:S(2)}) async-start(bf16[16,8,512]{2,1,0:T(8,128)(2,1)} %bitcast.2), calls=%async_computation | async-start | bytes 262144 | tf_op jit(solution)/shard_map/all_to_all | solution.py:260

commit v7 on v6

--- a/solution.py
+++ b/solution.py
@@ -150,7 +150,9 @@
     for at, pair in enumerate(pairs):
         rows = (me ^ jnp.where(core == 0, pair[0], pair[1])) * seqs
         t[pl.ds(pl.multiple_of(rows, 16), seqs), :] = part[at * seqs:(at + 1) * seqs].astype(t.dtype)
-    wanted = lax.broadcasted_iota(jnp.int32, (total, total), 0)
+    at = lax.broadcasted_iota(jnp.int32, (total, total), 0)
+    each = seqs // 2
+    wanted = at % (total // 2) // each * seqs + at // (total // 2) * each + at % each
     pick = jnp.where(wanted == ids[...], 1.0, 0.0).astype(t.dtype)
     s_ref[...] = jnp.dot(pick, t[...], preferred_element_type=jnp.float32).astype(s_ref.dtype)
 
@@ -259,7 +261,7 @@
     part = partial_scores(pairs, facts, sequence_ids[None, :], mine, own_q, other_q)
     parts = lax.all_to_all(
         part.reshape(dp * cores, part.shape[0] // (dp * cores), -1),
-        ("dp", "mat"),
+        ("mat", "dp"),
         split_axis=0,
         concat_axis=0,
         tiled=True,

time: 37.9 us -> 37.6 us (level)
  no operation moved by 1% of the time
where the time goes in v7:
time: 37.6 us; the launch traced here: 37.4 us
  starting transfers between devices  16.4 us (44%)
  Pallas kernels  12.6 us (34%)
  waiting for transfers between devices  7.05 us (19%)
  between operations  0.73 us (2%)
  other arithmetic  0.63 us (2%)
    ppermute x4, starting transfers between devices, local(): lax.ppermute(piece, ('dp', 'mat'), [(d * 2 + c, (d ^ pair[c]) * 2 + c) fo...  8.78 us
    pallas_call x1, Pallas kernels, fisher_block(): pl.pallas_call(functools.partial(fisher_body, total), out_shape=jax.Shape...  6.8 us
    ppermute x4, waiting for transfers between devices, local(): lax.ppermute(piece, ('dp', 'mat'), [(d * 2 + c, (d ^ pair[c]) * 2 + c) fo...  6.21 us
    all_to_all x1, starting transfers between devices, local(): lax.all_to_all(part.reshape(dp * cores, part.shape[0] // (dp * cores), -1...  6.17 us
    pallas_call x1, Pallas kernels, load(): pl.pallas_call(functools.partial(load_body, pairs), out_shape=[pltpu.VMEM...  2.59 us
    pallas_call x1, Pallas kernels, partial_scores(): pl.pallas_call(functools.partial(score_body, pairs), out_shape=jax.ShapeD...  2.21 us
    pallas_call x1, Pallas kernels, whole_slots(): pl.pallas_call(functools.partial(whole_body, n), out_shape=[pltpu.VMEM((s...  1.02 us
    all_to_all x1, waiting for transfers between devices, local(): lax.all_to_all(part.reshape(dp * cores, part.shape[0] // (dp * cores), -1...  0.82 us
  transfers between devices with their start and end apart: 11, of which 4 were waited for; matrix products, arithmetic and copies ran while one was open for 0% of the time, Pallas kernels for 31%

profile of v7, /device:TPU:0, one launch (start us, length us, event | category | flops | bytes accessed | tf_op | source)
XLA Modules:
  0.0 37.4 jit_solution(11889132157810748367)
XLA Ops:
  0.6 0.5 %collective-permute-start = (bf16[16,8,32,128]{3,2,1,0:T(8,128)(2,1)}, bf16[16,8,32,128]{3,2,1,0:T(8,128)(2,1)S(1)}, u32[]{:S(2)}, u32[]{:S(2)}) collective-permute-start(bf16[16,8,32,128]{3,2,1,0:T(8,128)(2,1)} %refs_0_.1), channel_id=1, source_target_pairs={{0,1},{1,0},{2,3},{3,2},{4,5},{5,4},{6,7},{7,6},{8,9},{9,8},{10,11... | collective-permute-start | bytes 3145736 | tf_op jit(solution)/shard_map/ppermute | solution.py:248
  1.1 2.6 %load.1 = (bf16[16,8,32,128]{3,2,1,0:T(8,128)(2,1)S(1)}, bf16[16,8,64,128]{3,2,1,0:T(8,128)(2,1)S(1)}, bf16[512,2048]{1,0:T(8,128)(2,1)S(1)}, s32[22]{0:T(128)S(4)}) custom-call(s32[8]{0:T(128)} %owner_hbm.1, s32[16]{0:T(128)} %lengths_hbm.1, bf16[16,8,32,128]{3,2,1,0:T(8,128)(2,1)} %refs_0_.1, bf16[16,8,64,128]{3,2,1,0:T(8,128)(2,1)} %refs_1_.1, ...), custom_call_target="tpu_custom_call" | custom-call | tf_op jit(solution)/shard_map/load/pallas_call | solution.py:86
  3.7 0.0 collective-permute-done.other_v
  3.8 0.0 copy-start
  3.8 1.0 %whole_slots.1 = (bf16[16,4096]{1,0:T(8,128)(2,1)S(1)}, bf16[16,4096]{1,0:T(8,128)(2,1)S(1)}, bf16[16,4096]{1,0:T(8,128)(2,1)S(1)}, bf16[16,4096]{1,0:T(8,128)(2,1)S(1)}, bf16[512,2048]{1,0:T(8,128)(2,1)S(1)}) custom-call(s32[22]{0:T(128)S(4)} %get-tuple-element.11.facts, ...), custom_call_target="tpu_custom_call", output_to_operand_aliasing={{4}: (4, {})} | custom-call | flops 67108864 | bytes 2097152 | tf_op jit(solution)/shard_map/whole_slots/pallas_call | solution.py:118
  4.8 0.3 collective-permute-start.9
  5.1 3.9 %collective-permute-start.1 = (bf16[16,4096]{1,0:T(8,128)(2,1)S(1)}, bf16[16,4096]{1,0:T(8,128)(2,1)S(1)}, u32[]{:S(2)}, u32[]{:S(2)}) collective-permute-start(bf16[16,4096]{1,0:T(8,128)(2,1)S(1)} %get-tuple-element.15), channel_id=1, source_target_pairs={{0,8},{1,11},{2,10},{3,9},{4,12},{5,15},{6,14},{7,13},{8,0},{9,3},... | collective-permute-start | bytes 393224 | tf_op jit(solution)/shard_map/ppermute | solution.py:254
  9.0 2.5 %collective-permute-start.2 = (bf16[16,4096]{1,0:T(8,128)(2,1)S(1)}, bf16[16,4096]{1,0:T(8,128)(2,1)S(1)}, u32[]{:S(2)}, u32[]{:S(2)}) collective-permute-start(bf16[16,4096]{1,0:T(8,128)(2,1)S(1)} %get-tuple-element.16), channel_id=1, source_target_pairs={{0,6},{1,5},{2,4},{3,7},{4,2},{5,1},{6,0},{7,3},{8,14},{9,13},{10,... | collective-permute-start | bytes 393224 | tf_op jit(solution)/shard_map/ppermute | solution.py:254
  11.5 0.2 collective-permute-start.3
  11.7 2.2 %collective-permute-start.4 = (bf16[16,4096]{1,0:T(8,128)(2,1)S(1)}, bf16[16,4096]{1,0:T(8,128)(2,1)S(1)}, u32[]{:S(2)}, u32[]{:S(2)}) collective-permute-start(bf16[16,4096]{1,0:T(8,128)(2,1)S(1)} %get-tuple-element.18), channel_id=1, source_target_pairs={{0,2},{1,1},{2,0},{3,3},{4,6},{5,5},{6,4},{7,7},{8,10},{9,9},{10,8... | collective-permute-start | bytes 393224 | tf_op jit(solution)/shard_map/ppermute | solution.py:254
  13.9 1.8 %collective-permute-done.1.refs_0_ = bf16[16,4096]{1,0:T(8,128)(2,1)S(1)} collective-permute-done((bf16[16,4096]{1,0:T(8,128)(2,1)S(1)}, bf16[16,4096]{1,0:T(8,128)(2,1)S(1)}, u32[]{:S(2)}, u32[]{:S(2)}) %collective-permute-start.1) | collective-permute-done | bytes 131104 | tf_op jit(solution)/shard_map/ppermute | solution.py:254
  15.7 0.1 collective-permute-start.5
  15.8 0.7 %collective-permute-done.2.refs_1_ = bf16[16,4096]{1,0:T(8,128)(2,1)S(1)} collective-permute-done((bf16[16,4096]{1,0:T(8,128)(2,1)S(1)}, bf16[16,4096]{1,0:T(8,128)(2,1)S(1)}, u32[]{:S(2)}, u32[]{:S(2)}) %collective-permute-start.2) | collective-permute-done | bytes 131104 | tf_op jit(solution)/shard_map/ppermute | solution.py:254
  16.5 0.0 collective-permute-start.6
  16.5 3.7 %collective-permute-done.3.refs_2_ = bf16[16,4096]{1,0:T(8,128)(2,1)S(1)} collective-permute-done((bf16[16,4096]{1,0:T(8,128)(2,1)S(1)}, bf16[16,4096]{1,0:T(8,128)(2,1)S(1)}, u32[]{:S(2)}, u32[]{:S(2)}) %collective-permute-start.3) | collective-permute-done | bytes 131104 | tf_op jit(solution)/shard_map/ppermute | solution.py:254
  20.2 0.0 collective-permute-start.7
  20.2 0.0 collective-permute-done.4.refs_3_
  20.2 0.5 %collective-permute-start.8 = (bf16[16,4096]{1,0:T(8,128)(2,1)S(1)}, bf16[16,4096]{1,0:T(8,128)(2,1)S(1)}, u32[]{:S(2)}, u32[]{:S(2)}) collective-permute-start(bf16[16,4096]{1,0:T(8,128)(2,1)S(1)} %collective-permute-done.4.refs_3_), channel_id=1, source_target_pairs={{0,1},{1,0},{2,3},{3,2},{4,5},{5,4},{6,7},{7,6},{8,9},{9,8},{10,11... | collective-permute-start | bytes 393224 | tf_op jit(solution)/shard_map/ppermute | solution.py:260
  20.7 0.0 collective-permute-done.9.refs_5_
  20.7 0.0 copy-done
  20.7 2.2 %scores.1 = bf16[128,512]{1,0:T(8,128)(2,1)} custom-call(s32[22]{0:T(128)S(4)} %get-tuple-element.11.facts, s32[1,128]{1,0:T(1,128)S(1)} %bitcast.3, bf16[16,4096]{1,0:T(8,128)(2,1)S(1)} %collective-permute-done.1.refs_0_, bf16[16,4096]{1,0:T(8,128)(2,1)S(1)} %collective-permute-done.2.refs_1_, bf16[16,4096]{1,0:T(8,128)(2,1)S(1)} %collective-permute-done.3.refs_2_, ...), custom_call_target="tpu_custom_call" | custom-call | flops 268435456 | bytes 4718592 | tf_op jit(solution)/shard_map/scores/pallas_call | solution.py:166
  22.9 6.2 %all-to-all-start = ((bf16[16,8,512]{2,1,0:T(8,128)(2,1)}), bf16[16,8,512]{2,1,0:T(8,128)(2,1)S(1)}, u32[]{:S(2)}, u32[]{:S(2)}) async-start(bf16[16,8,512]{2,1,0:T(8,128)(2,1)} %bitcast.2), calls=%async_computation | async-start | bytes 262144 | tf_op jit(solution)/shard_map/all_to_all | solution.py:262
  29.1 0.0 collective-permute-done.5.refs_4_
  29.1 0.0 collective-permute-done.6.refs_5_
  29.1 0.0 collective-permute-done.7.refs_6_
  29.1 0.0 collective-permute-done.8.refs_7_
  29.1 6.8 %fisher.1 = bf16[1,2048,4096]{2,1,0:T(8,128)(2,1)} custom-call(s32[22]{0:T(128)S(4)} %get-tuple-element.11.facts, bf16[16,4096]{1,0:T(8,128)(2,1)S(1)} %collective-permute-done.1.refs_0_, bf16[16,4096]{1,0:T(8,128)(2,1)S(1)} %collective-permute-done.2.refs_1_, bf16[16,4096]{1,0:T(8,128)(2,1)S(1)} %collective-permute-done.3.refs_2_, ...), custom_call_target="tpu_custom_call" | custom-call | flops 2147483648 | bytes 17825792 | tf_op jit(solution)/shard_map/fisher/pallas_call | solution.py:221
  35.9 0.8 %all-to-all-done = bf16[16,8,512]{2,1,0:T(8,128)(2,1)S(1)} async-done(((bf16[16,8,512]{2,1,0:T(8,128)(2,1)}), bf16[16,8,512]{2,1,0:T(8,128)(2,1)S(1)}, u32[]{:S(2)}, u32[]{:S(2)}) %all-to-all-start) | async-done | bytes 131104 | tf_op jit(solution)/shard_map/all_to_all | solution.py:262
  36.8 0.6 %convert_reduce_fusion = f32[8,512]{1,0:T(8,128)} fusion(bf16[16,8,512]{2,1,0:T(8,128)(2,1)S(1)} %all-to-all-done), kind=kLoop, calls=%fused_computation | loop fusion | flops 126976 | bytes 147456 | tf_op jit(solution)/shard_map/reduce_sum | solution.py:270
Async XLA Ops:
  0.6 3.1 %collective-permute-start = (bf16[16,8,32,128]{3,2,1,0:T(8,128)(2,1)}, bf16[16,8,32,128]{3,2,1,0:T(8,128)(2,1)S(1)}, u32[]{:S(2)}, u32[]{:S(2)}) collective-permute-start(bf16[16,8,32,128]{3,2,1,0:T(8,128)(2,1)} %refs_0_.1), channel_id=1, source_target_pairs={{0,1},{1,0},{2,3},{3,2},{4,5},{5,4},{6,7},{7,6},{8,9},{9,8},{10,11... | collective-permute-start | bytes 3145736 | tf_op jit(solution)/shard_map/ppermute | solution.py:248
  3.8 16.9 %copy-start = (s32[128]{0:T(128)S(1)}, s32[128]{0:T(128)}, u32[]{:S(2)}) copy-start(s32[128]{0:T(128)} %param.9) | copy-start | bytes 1540
  4.8 15.9 %collective-permute-start.9 = (bf16[512,2048]{1,0:T(8,128)(2,1)S(1)}, bf16[512,2048]{1,0:T(8,128)(2,1)S(1)}, u32[]{:S(2)}, u32[]{:S(2)}) collective-permute-start(bf16[512,2048]{1,0:T(8,128)(2,1)S(1)} %get-tuple-element.19.refs_4_), channel_id=1, source_target_pairs={{0,1},{1,0},{2,3},{3,2},{4,5},{5,4},{6,7},{7,6},{8,9},{9,8},{10,11... | collective-permute-start | bytes 6291464 | tf_op jit(solution)/shard_map/ppermute | solution.py:259
  5.1 10.6 %collective-permute-start.1 = (bf16[16,4096]{1,0:T(8,128)(2,1)S(1)}, bf16[16,4096]{1,0:T(8,128)(2,1)S(1)}, u32[]{:S(2)}, u32[]{:S(2)}) collective-permute-start(bf16[16,4096]{1,0:T(8,128)(2,1)S(1)} %get-tuple-element.15), channel_id=1, source_target_pairs={{0,8},{1,11},{2,10},{3,9},{4,12},{5,15},{6,14},{7,13},{8,0},{9,3},... | collective-permute-start | bytes 393224 | tf_op jit(solution)/shard_map/ppermute | solution.py:254
  9.0 7.5 %collective-permute-start.2 = (bf16[16,4096]{1,0:T(8,128)(2,1)S(1)}, bf16[16,4096]{1,0:T(8,128)(2,1)S(1)}, u32[]{:S(2)}, u32[]{:S(2)}) collective-permute-start(bf16[16,4096]{1,0:T(8,128)(2,1)S(1)} %get-tuple-element.16), channel_id=1, source_target_pairs={{0,6},{1,5},{2,4},{3,7},{4,2},{5,1},{6,0},{7,3},{8,14},{9,13},{10,... | collective-permute-start | bytes 393224 | tf_op jit(solution)/shard_map/ppermute | solution.py:254
  11.5 8.7 %collective-permute-start.3 = (bf16[16,4096]{1,0:T(8,128)(2,1)S(1)}, bf16[16,4096]{1,0:T(8,128)(2,1)S(1)}, u32[]{:S(2)}, u32[]{:S(2)}) collective-permute-start(bf16[16,4096]{1,0:T(8,128)(2,1)S(1)} %get-tuple-element.17), channel_id=1, source_target_pairs={{0,12},{1,15},{2,14},{3,13},{4,8},{5,11},{6,10},{7,9},{8,4},{9,7},... | collective-permute-start | bytes 393224 | tf_op jit(solution)/shard_map/ppermute | solution.py:254
  11.7 8.5 %collective-permute-start.4 = (bf16[16,4096]{1,0:T(8,128)(2,1)S(1)}, bf16[16,4096]{1,0:T(8,128)(2,1)S(1)}, u32[]{:S(2)}, u32[]{:S(2)}) collective-permute-start(bf16[16,4096]{1,0:T(8,128)(2,1)S(1)} %get-tuple-element.18), channel_id=1, source_target_pairs={{0,2},{1,1},{2,0},{3,3},{4,6},{5,5},{6,4},{7,7},{8,10},{9,9},{10,8... | collective-permute-start | bytes 393224 | tf_op jit(solution)/shard_map/ppermute | solution.py:254
  15.7 13.4 %collective-permute-start.5 = (bf16[16,4096]{1,0:T(8,128)(2,1)S(1)}, bf16[16,4096]{1,0:T(8,128)(2,1)S(1)}, u32[]{:S(2)}, u32[]{:S(2)}) collective-permute-start(bf16[16,4096]{1,0:T(8,128)(2,1)S(1)} %collective-permute-done.1.refs_0_), channel_id=1, source_target_pairs={{0,1},{1,0},{2,3},{3,2},{4,5},{5,4},{6,7},{7,6},{8,9},{9,8},{10,11... | collective-permute-start | bytes 393224 | tf_op jit(solution)/shard_map/ppermute | solution.py:260
  16.5 12.6 %collective-permute-start.6 = (bf16[16,4096]{1,0:T(8,128)(2,1)S(1)}, bf16[16,4096]{1,0:T(8,128)(2,1)S(1)}, u32[]{:S(2)}, u32[]{:S(2)}) collective-permute-start(bf16[16,4096]{1,0:T(8,128)(2,1)S(1)} %collective-permute-done.2.refs_1_), channel_id=1, source_target_pairs={{0,1},{1,0},{2,3},{3,2},{4,5},{5,4},{6,7},{7,6},{8,9},{9,8},{10,11... | collective-permute-start | bytes 393224 | tf_op jit(solution)/shard_map/ppermute | solution.py:260
  20.2 8.9 %collective-permute-start.7 = (bf16[16,4096]{1,0:T(8,128)(2,1)S(1)}, bf16[16,4096]{1,0:T(8,128)(2,1)S(1)}, u32[]{:S(2)}, u32[]{:S(2)}) collective-permute-start(bf16[16,4096]{1,0:T(8,128)(2,1)S(1)} %collective-permute-done.3.refs_2_), channel_id=1, source_target_pairs={{0,1},{1,0},{2,3},{3,2},{4,5},{5,4},{6,7},{7,6},{8,9},{9,8},{10,11... | collective-permute-start | bytes 393224 | tf_op jit(solution)/shard_map/ppermute | solution.py:260
  20.2 8.9 %collective-permute-start.8 = (bf16[16,4096]{1,0:T(8,128)(2,1)S(1)}, bf16[16,4096]{1,0:T(8,128)(2,1)S(1)}, u32[]{:S(2)}, u32[]{:S(2)}) collective-permute-start(bf16[16,4096]{1,0:T(8,128)(2,1)S(1)} %collective-permute-done.4.refs_3_), channel_id=1, source_target_pairs={{0,1},{1,0},{2,3},{3,2},{4,5},{5,4},{6,7},{7,6},{8,9},{9,8},{10,11... | collective-permute-start | bytes 393224 | tf_op jit(solution)/shard_map/ppermute | solution.py:260
  22.9 13.8 %all-to-all-start = ((bf16[16,8,512]{2,1,0:T(8,128)(2,1)}), bf16[16,8,512]{2,1,0:T(8,128)(2,1)S(1)}, u32[]{:S(2)}, u32[]{:S(2)}) async-start(bf16[16,8,512]{2,1,0:T(8,128)(2,1)} %bitcast.2), calls=%async_computation | async-start | bytes 262144 | tf_op jit(solution)/shard_map/all_to_all | solution.py:262
